TPU v7x, 32 devices: a whole 2x2x4 slice. The times are simulated.
32 devices in a mesh: scen: 8 (over y, x, core), grp: 4 (over z).
Axes of the slice: x: 2, y: 2, z: 4, core: 2. Of those that a mesh axis runs over, the one named last changes fastest.
Arguments:
- coupling: bfloat16 [32, 768, 4096], P(('scen', 'grp')), may hold values from -1.5 to 1.5
- scen_kkt: bfloat16 [32, 768, 768], P(('scen', 'grp')), may hold values from -3 to 5, as said below
- active_rows: int32 [32], P(('scen', 'grp')), may hold values from 128 to 768, as said below
- first_hess: float32 [512], replicated, may hold values from 20 to 400
Outputs:
- factor_panels: float32 [4096, 512], P('scen')
Inputs may be any that keep to these rules, and one draw needn't show every extreme that they name: `scen_kkt`: each block is symmetric positive definite: a Gram matrix of 768 columns divided by 768 plus a positive diagonal. `active_rows`: each count is a multiple of 128; some scenario has 768 and some has 128.
All inputs are finite; a program needn't handle non-finite values.
Results may differ from a plain program's by a relative error of at most 0.0011.
Values sent between devices are 32-bit elements; how exact they have to be, the bound alone decides.
No kernel may reach another device: no remote copies, remote signals or barrier semaphores. Data moves between devices by JAX's collectives and lax.ppermute only.
A program may use at most 64 MiB of HBM per device.

v0:
```python
import jax
import jax.numpy as jnp
from jax import lax
from jax.sharding import PartitionSpec as P

PW = 256


def from_root(block, axis, holder):
    block = jnp.where(lax.axis_index(axis) == holder, block, jnp.zeros_like(block))
    return lax.psum(block, axis)


def solve_block(factor, right_side):
    return jax.scipy.linalg.cho_solve((factor, True), right_side)


def solve_right(lower_tri, rows):
    return jax.scipy.linalg.solve_triangular(lower_tri, rows.T, lower=True).T


def from_owners(local_rows, span_lo, span_hi, own_rows, sender):
    pieces = []
    for owner_idx in range(span_lo // own_rows, (span_hi - 1) // own_rows + 1):
        pieces.append(sender(local_rows, owner_idx))
    return jax.tree.map(lambda *arrays: jnp.concatenate(arrays, 0), *pieces)


def per_device(coupling, scen_kkt, active_rows, first_hess):
    count_sc, rows_sc, coupled = coupling.shape
    n_scen = lax.axis_size("scen")
    own_rows = coupled // n_scen
    scen_idx = lax.axis_index("scen")
    panel_cols = 2 * PW
    tile_pos = lax.broadcasted_iota(jnp.int32, (count_sc, rows_sc, 1), 1)
    keep_mask = (tile_pos < active_rows[:, None, None]).astype(jnp.float32)
    coupling_panel = coupling[:, :, :panel_cols].astype(jnp.float32) * keep_mask
    factor = jnp.linalg.cholesky(scen_kkt.astype(jnp.float32))
    solved = (jax.vmap(solve_block)(factor, coupling_panel) * keep_mask).astype(jnp.bfloat16)
    own_panel = lax.psum_scatter(
        jnp.einsum("snr,snc->rc", coupling, solved, preferred_element_type=jnp.float32),
        "scen",
        scatter_dimension=0,
        tiled=True,
    )
    own_panel = lax.psum(own_panel, "grp")
    global_row = scen_idx * own_rows + lax.broadcasted_iota(jnp.int32, (own_rows, 1), 0)
    col_ids = lax.broadcasted_iota(jnp.int32, (1, panel_cols), 1)
    own_panel = own_panel + jnp.where(global_row == col_ids, first_hess[None, :], 0.0)
    pivot_panel = from_owners(
        own_panel,
        0,
        2 * PW,
        own_rows,
        lambda row_slab, root_idx: from_root(row_slab, "scen", root_idx),
    )
    diag_one = jnp.linalg.cholesky(pivot_panel[:PW, :PW])
    mid_lower = solve_right(diag_one, pivot_panel[PW:, :PW])
    mid_panel = pivot_panel[PW:, PW:]
    lower_own = solve_right(diag_one, own_panel[:, :PW])
    updated_mid = mid_panel - jnp.dot(
        mid_lower, mid_lower.T, precision=lax.Precision.HIGHEST, preferred_element_type=jnp.float32
    )
    diag_two = jnp.linalg.cholesky(updated_mid)
    updated_own = own_panel[:, PW:] - jnp.dot(
        lower_own, mid_lower.T, precision=lax.Precision.HIGHEST, preferred_element_type=jnp.float32
    )
    lower_two = solve_right(diag_two, updated_own)
    zero_rows = jnp.zeros((own_rows, PW), jnp.float32)
    start_one = jnp.minimum(scen_idx * own_rows, PW)
    take_one = lax.dynamic_slice_in_dim(
        jnp.concatenate([diag_one, zero_rows], 0), start_one, own_rows, 0
    )
    left_half = jnp.where(global_row < PW, take_one, lower_own)
    start_two = jnp.minimum(scen_idx * own_rows, 2 * PW)
    padded_two = jnp.concatenate([jnp.zeros((PW, PW), jnp.float32), diag_two, zero_rows], 0)
    take_two = lax.dynamic_slice_in_dim(padded_two, start_two, own_rows, 0)
    right_half = jnp.where(global_row < 2 * PW, take_two, lower_two)
    return jnp.concatenate([left_half, right_half], 1)


def solution(mesh):
    placed = (
        P(("scen", "grp"), None, None),
        P(("scen", "grp"), None, None),
        P(("scen", "grp")),
        P(),
    )
    return jax.shard_map(
        per_device, mesh=mesh, in_specs=placed, out_specs=P("scen", None), check_vma=False
    )
```

profile of v0, /device:TPU:0, one launch (start us, length us, event | category | flops | bytes accessed | tf_op | source)
XLA Modules:
  0.0 576.3 jit_solution(3081377300929240434)
XLA Ops:
  6.5 1.6 copy.5
  9.0 1.4 copy-done.1
  10.4 11.7 %custom-call.71 = f32[1,128,128]{2,1,0:T(8,128)S(1)} custom-call(f32[1,128,128]{2,1,0:T(8,128)S(1)} %cholesky.621), custom_call_target="Cholesky" | custom-call | tf_op jit(solution)/shard_map/jit(cholesky)/cholesky | solution.py:38
  22.2 9.8 %custom-call.72 = f32[1,1,128,128]{2,3,1,0:T(8,128)S(1)} custom-call(f32[1,1,128,128]{3,2,1,0:T(8,128)S(1)} %get-tuple-element.100), custom_call_target="InvertDiagBlocksLowerTriangular" | custom-call | tf_op jit(solution)/shard_map/jit(cholesky)/cholesky | solution.py:38
  32.2 1.4 constant_dynamic-update-slice_fusion.15
  33.5 1.4 fusion.7
  35.0 11.7 %custom-call.73 = f32[1,128,128]{2,1,0:T(8,128)S(1)} custom-call(f32[1,128,128]{2,1,0:T(8,128)S(1)} %cholesky.625), custom_call_target="Cholesky" | custom-call | tf_op jit(solution)/shard_map/jit(cholesky)/cholesky | solution.py:38
  46.7 10.1 %custom-call.74 = f32[1,1,128,128]{2,3,1,0:T(8,128)S(1)} custom-call(f32[1,1,128,128]{3,2,1,0:T(8,128)S(1)} %get-tuple-element.97), custom_call_target="InvertDiagBlocksLowerTriangular" | custom-call | tf_op jit(solution)/shard_map/jit(cholesky)/cholesky | solution.py:38
  57.2 1.5 fusion.18
  58.7 11.7 %custom-call.75 = f32[1,128,128]{2,1,0:T(8,128)S(1)} custom-call(f32[1,128,128]{2,1,0:T(8,128)S(1)} %cholesky.630), custom_call_target="Cholesky" | custom-call | tf_op jit(solution)/shard_map/jit(cholesky)/cholesky | solution.py:38
  71.1 9.8 %custom-call.76 = f32[1,1,128,128]{2,3,1,0:T(8,128)S(1)} custom-call(f32[1,1,128,128]{3,2,1,0:T(8,128)S(1)} %get-tuple-element.94), custom_call_target="InvertDiagBlocksLowerTriangular" | custom-call | tf_op jit(solution)/shard_map/jit(cholesky)/cholesky | solution.py:38
  81.3 1.6 fusion.32
  82.8 11.9 %custom-call.77 = f32[1,128,128]{2,1,0:T(8,128)S(1)} custom-call(f32[1,128,128]{2,1,0:T(8,128)S(1)} %cholesky.635), custom_call_target="Cholesky" | custom-call | tf_op jit(solution)/shard_map/jit(cholesky)/cholesky | solution.py:38
  95.5 9.8 %custom-call.78 = f32[1,1,128,128]{2,3,1,0:T(8,128)S(1)} custom-call(f32[1,1,128,128]{3,2,1,0:T(8,128)S(1)} %get-tuple-element.91), custom_call_target="InvertDiagBlocksLowerTriangular" | custom-call | tf_op jit(solution)/shard_map/jit(cholesky)/cholesky | solution.py:38
  105.5 1.5 fusion.34
  107.0 11.7 %custom-call.79 = f32[1,128,128]{2,1,0:T(8,128)S(1)} custom-call(f32[1,128,128]{2,1,0:T(8,128)S(1)} %cholesky.640), custom_call_target="Cholesky" | custom-call | tf_op jit(solution)/shard_map/jit(cholesky)/cholesky | solution.py:38
  119.4 9.8 %custom-call.80 = f32[1,1,128,128]{2,3,1,0:T(8,128)S(1)} custom-call(f32[1,1,128,128]{3,2,1,0:T(8,128)S(1)} %get-tuple-element.88), custom_call_target="InvertDiagBlocksLowerTriangular" | custom-call | tf_op jit(solution)/shard_map/jit(cholesky)/cholesky | solution.py:38
  129.4 1.3 fusion.36
  130.8 12.1 %custom-call.81 = f32[1,128,128]{2,1,0:T(8,128)S(1)} custom-call(f32[1,128,128]{2,1,0:T(8,128)S(1)} %fusion.36), custom_call_target="Cholesky" | custom-call | tf_op jit(solution)/shard_map/jit(cholesky)/cholesky | solution.py:38
  148.0 1.6 select_select_fusion
  149.6 21.6 %while.6 = (s32[]{:T(128)}, f32[1,768,768]{2,1,0:T(8,128)}, s32[6,2]{0,1:T(2,128)S(1)}, f32[6,1,128,128]{3,2,1,0:T(8,128)}, s32[]{:T(128)}) while((s32[]{:T(128)}, f32[1,768,768]{2,1,0:T(8,128)}, s32[6,2]{0,1:T(2,128)S(1)}, f32[6,1,128,128]{3,2,1,0:T(8,128)}, s32[]{:T(128)}) %tuple.81), condition=%wide.while_cond.1, body=%wide.while_body.1.sunk | while | flops 2 | bytes 132705 | solution.py:15
  150.3 2.9 bitcast_dynamic-update-slice_fusion.13
  153.9 2.9 bitcast_dynamic-update-slice_fusion.13
  157.5 2.9 bitcast_dynamic-update-slice_fusion.13
  161.1 2.9 bitcast_dynamic-update-slice_fusion.13
  164.7 2.9 bitcast_dynamic-update-slice_fusion.13
  168.3 2.9 bitcast_dynamic-update-slice_fusion.13
  171.2 59.9 %custom-call.82 = f32[1,6,128,128]{2,3,1,0:T(8,128)S(1)} custom-call(f32[1,6,128,128]{3,2,1,0:T(8,128)} %bitcast.424), custom_call_target="InvertDiagBlocksLowerTriangular" | custom-call | tf_op jit(solution)/shard_map/vmap(jit(_cho_solve))/triangular_solve | solution.py:15
  231.8 1.3 convert_multiply_fusion
  244.6 5.9 %convolution_bitcast_fusion = f32[4096,512]{0,1:T(8,128)} fusion(bf16[1,768,4096]{2,1,0:T(8,128)(2,1)S(1)} %bitcast.407, f32[1,768,1,1,1,1,512]{6,1,5,4,3,2,0:T(8,128)S(1)} %bitcast_dynamic-update-slice_fusion.3, f32[768]{0:T(1024)S(1)} %fusion.107), kind=kOutput, calls=%fused_computation.6 | convolution fusion | flops 3222011904 | bytes 16256000 | tf_op jit(solution)/shard_map/snr,snc->rc/dot_general | solution.py:41
  250.7 74.1 %reduce-scatter.2.cloned.1.call-done = f32[512,512]{0,1:T(8,128)} async-done(((f32[4096,512]{0,1:T(8,128)}), f32[512,512]{0,1:T(8,128)}) %reduce-scatter.2.cloned.1.call-update) | async-done | bytes 1048592 | tf_op jit(solution)/shard_map/reduce_scatter | solution.py:40
  325.0 54.1 %all-reduce.6.cloned.1.call-done = f32[512,512]{0,1:T(8,128)} async-done(((f32[512,512]{0,1:T(8,128)}), f32[512,512]{0,1:T(8,128)}) %all-reduce.6.cloned.1.call-update) | async-done | bytes 1048592 | tf_op jit(solution)/shard_map/psum | solution.py:46
  379.0 2.5 broadcast_select_fusion
  381.7 56.5 %all-reduce.8.cloned.1.call-done = f32[512,512]{0,1:T(8,128)} async-done(((f32[512,512]{0,1:T(8,128)}), f32[512,512]{0,1:T(8,128)}) %all-reduce.8.cloned.1.call-update) | async-done | bytes 1048592 | tf_op jit(solution)/shard_map/psum | solution.py:11
  440.4 11.7 %cholesky.557 = f32[128,128]{1,0:T(8,128)S(1)} custom-call(f32[128,128]{1,0:T(8,128)S(1)} %cholesky.644), custom_call_target="Cholesky" | custom-call | tf_op jit(solution)/shard_map/jit(cholesky)/cholesky | solution.py:57
  452.2 9.8 %custom-call.86 = f32[1,128,128]{1,2,0:T(8,128)S(1)} custom-call(f32[1,128,128]{2,1,0:T(8,128)S(1)} %get-tuple-element.84), custom_call_target="InvertDiagBlocksLowerTriangular" | custom-call | tf_op jit(solution)/shard_map/jit(cholesky)/cholesky | solution.py:57
  462.7 11.7 %cholesky.574 = f32[128,128]{1,0:T(8,128)S(1)} custom-call(f32[128,128]{1,0:T(8,128)S(1)} %convolution_subtract_fusion.10), custom_call_target="Cholesky" | custom-call | tf_op jit(solution)/shard_map/jit(cholesky)/cholesky | solution.py:57
  477.1 3.8 while.7
  479.6 1.3 bitcast_dynamic-update-slice_fusion.14
  480.9 19.9 %custom-call.87 = f32[2,128,128]{1,2,0:T(8,128)S(1)} custom-call(f32[2,128,128]{2,1,0:T(8,128)S(1)} %get-tuple-element.37), custom_call_target="InvertDiagBlocksLowerTriangular" | custom-call | tf_op jit(solution)/shard_map/jit(_solve_triangular)/triangular_solve | solution.py:19
  503.3 1.5 convolution_subtract_fusion.2
  505.0 11.7 %cholesky.591 = f32[128,128]{1,0:T(8,128)S(1)} custom-call(f32[128,128]{1,0:T(8,128)S(1)} %cholesky.647), custom_call_target="Cholesky" | custom-call | tf_op jit(solution)/shard_map/jit(cholesky)/cholesky | solution.py:64
  516.8 9.8 %custom-call.88 = f32[1,128,128]{1,2,0:T(8,128)S(1)} custom-call(f32[1,128,128]{2,1,0:T(8,128)S(1)} %get-tuple-element.80), custom_call_target="InvertDiagBlocksLowerTriangular" | custom-call | tf_op jit(solution)/shard_map/jit(cholesky)/cholesky | solution.py:64
  527.1 11.9 %cholesky.608 = f32[128,128]{1,0:T(8,128)S(1)} custom-call(f32[128,128]{1,0:T(8,128)S(1)} %convolution_subtract_fusion.9), custom_call_target="Cholesky" | custom-call | tf_op jit(solution)/shard_map/jit(cholesky)/cholesky | solution.py:64
  541.8 4.1 while.8
  542.4 1.4 bitcast_dynamic-update-slice_fusion.15
  544.5 1.4 bitcast_dynamic-update-slice_fusion.15
  545.9 19.7 %custom-call.89 = f32[2,128,128]{1,2,0:T(8,128)S(1)} custom-call(f32[2,128,128]{2,1,0:T(8,128)S(1)} %get-tuple-element.38), custom_call_target="InvertDiagBlocksLowerTriangular" | custom-call | tf_op jit(solution)/shard_map/jit(_solve_triangular)/triangular_solve | solution.py:19
  (145 shorter events, 37.7 us)
Async XLA Ops:
  6.5 318.2 %reduce-scatter.2.cloned.1.call-start = ((), (), s32[]{:S(2)}) async-start(), calls=%async_computation.1 | async-start | bytes 9437184 | tf_op jit(solution)/shard_map/reduce_scatter | solution.py:40
  9.0 1.4 copy-start.1
  171.2 62.3 %copy-start = (f32[1,768,768]{2,1,0:T(8,128)S(1)}, f32[1,768,768]{2,1,0:T(8,128)}, u32[]{:S(2)}) copy-start(f32[1,768,768]{2,1,0:T(8,128)} %get-tuple-element.258) | copy-start | bytes 7077892
  239.2 5.4 slice-start
  242.6 2.0 slice-start.1
  250.6 128.5 %copy-start.2 = (f32[512]{0:T(512)S(1)}, f32[512]{0:T(512)}, u32[]{:S(2)}) copy-start(f32[512]{0:T(512)} %param.10) | copy-start | bytes 6148
  250.6 128.4 %all-reduce.6.cloned.1.call-start = ((), (), s32[]{:S(2)}) async-start(), calls=%async_computation.2 | async-start | bytes 2097152 | tf_op jit(solution)/shard_map/psum | solution.py:46
  324.7 113.5 %all-reduce.8.cloned.1.call-start = ((), (), s32[]{:S(2)}) async-start(), calls=%async_computation.3 | async-start | bytes 2097152 | tf_op jit(solution)/shard_map/psum | solution.py:11
Sparse Core Ops, SparseCore 0:
  250.7 73.9 reduce-scatter.1
  327.2 51.7 all-reduce.5
  382.2 55.9 all-reduce.7
where the time goes:
time: 586 us; the launch traced here: 576 us
  other arithmetic  301 us (51%)
  waiting for transfers between devices  185 us (32%)
  local copies, waits for them, and re-layouts  35.4 us (6%)
  matrix products  33.7 us (6%)
  between operations  21.4 us (4%)
    another operation x22, other arithmetic, per_device(): factor = jnp.linalg.cholesky(scen_kkt.astype(jnp.float32))  124 us
    reduce_scatter x1, waiting for transfers between devices, per_device(): lax.psum_scatter(jnp.einsum('snr,snc->rc', coupling, solved, preferred_el...  74.1 us
    another operation x3, other arithmetic, solve_block(): return jax.scipy.linalg.cho_solve((factor, True), right_side)  61.5 us
    psum x1, waiting for transfers between devices, from_root(): return lax.psum(block, axis)  56.5 us
    psum x1, waiting for transfers between devices, per_device(): own_panel = lax.psum(own_panel, 'grp')  54.1 us
    another operation x5, other arithmetic, solve_right(): return jax.scipy.linalg.solve_triangular(lower_tri, rows.T, lower=True).T  39.6 us
    another operation x7, other arithmetic, per_device(): diag_two = jnp.linalg.cholesky(updated_mid)  34.9 us
    another operation x7, other arithmetic, per_device(): diag_one = jnp.linalg.cholesky(pivot_panel[:PW, :PW])  34.6 us
  transfers between devices with their start and end apart: 3, of which 3 were waited for; matrix products, arithmetic and copies ran while one was open for 0% of the time, Pallas kernels for 0%

commit v1 on v0

v1 whole, which is shorter than its diff:
```python
import jax
import jax.numpy as jnp
from jax import lax
from jax.experimental import pallas as pl
from jax.experimental.pallas import tpu as pltpu
from jax.sharding import PartitionSpec as P

H=lax.Precision.HIGHEST
def bc(x,s): return jnp.broadcast_to(x[s:s+1,:], x.shape)
def elim(R, off, nb):
    ng=nb//8; nh=len(R[0])
    row=lax.broadcasted_iota(jnp.int32,(8,128),0)
    L={}
    for j in range(nb):
        for g in range(j//8,ng):
            L[j,g]=jnp.broadcast_to(R[g][0][:,off+j:off+j+1],(8,128))
    out=[]
    for g in range(ng): out.append(None)
    for j in range(0,nb,2):
        gj=j//8; s=j%8
        a=bc(L[j,gj],s); b=bc(L[j,gj],s+1); c=bc(L[j+1,gj],s+1)
        det=a*c-b*b
        rd=1.0/det
        al={}; be={}
        for g in range(gj,ng):
            x=L[j,g]*c-L[j+1,g]*b; y=L[j+1,g]*a-L[j,g]*b
            if g==gj:
                x=jnp.where(row>s+1,x,0.0); y=jnp.where(row>s+1,y,0.0)
            al[g]=x; be[g]=y
        for k in range(j+2,nb):
            p=bc(L[j,k//8],k%8); q=bc(L[j+1,k//8],k%8)
            for g in range(k//8,ng):
                L[k,g]=L[k,g]-(al[g]*p+be[g]*q)*rd
        r1=[bc(R[gj][h],s) for h in range(nh)]; r2=[bc(R[gj][h],s+1) for h in range(nh)]
        ra=1.0/a
        sa=lax.rsqrt(a); sb=lax.rsqrt(det*ra); ba=b*ra
        if s==0: out[gj]=[jnp.zeros((8,128),jnp.float32)]*nh
        for h in range(nh):
            out[gj][h]=jnp.where(row==s,r1[h]*sa,jnp.where(row==s+1,(r2[h]-ba*r1[h])*sb,out[gj][h]))
        for g in range(gj,ng):
            if g==gj and s==6: continue
            x=al[g]*rd; y=be[g]*rd
            R[g]=[R[g][h]-(x*r1[h]+y*r2[h]) for h in range(nh)]
    return out
def base128(A, nb=32, prec=H):
    row=lax.broadcasted_iota(jnp.int32,(8,128),0); lane=lax.broadcasted_iota(jnp.int32,(8,128),1)
    M=[[A[8*g:8*g+8,:],jnp.where(lane==row+8*g,1.0,0.0)] for g in range(16)]
    outs=[]
    n=128//nb; ng=nb//8
    for c in range(n):
        o=elim(M[c*ng:(c+1)*ng],c*nb,nb)
        outs+=o
        if c<n-1:
            O=[jnp.concatenate([o[g][h] for g in range(ng)],0) for h in range(2)]
            for h in range(2):
                T=lax.dot_general(O[0],O[h],(((0,),(0,)),((),())),precision=prec,preferred_element_type=jnp.float32)
                for g in range((c+1)*ng,16):
                    M[g][h]=M[g][h]-T[8*g:8*g+8]
    return [jnp.concatenate([outs[g][h] for g in range(16)],0) for h in range(2)]
def dotT(a,b,prec=H): return lax.dot_general(a,b,(((0,),(0,)),((),())),precision=prec,preferred_element_type=jnp.float32)
def dot(a,b,prec=H): return lax.dot_general(a,b,(((1,),(0,)),((),())),precision=prec,preferred_element_type=jnp.float32)
BS=128
def scen_kernel(act_ref,k_ref,c_ref,x_ref,A,Z,W):
    n=k_ref.shape[1]; nblk=n//BS
    act=act_ref[0]
    def keep(k):
        r=lax.broadcasted_iota(jnp.int32,(BS,1),0)+k*BS
        return r<act
    blk=lambda k: slice(k*BS,(k+1)*BS)
    for k in range(nblk):
        Akk=k_ref[0,blk(k),blk(k)].astype(jnp.float32) if k==0 else A[blk(k),blk(k)]
        _,Wk=base128(Akk)
        W[k]=Wk
        if k<nblk-1:
            src=k_ref[0,blk(k),(k+1)*BS:].astype(jnp.float32) if k==0 else A[blk(k),(k+1)*BS:]
            P=dot(Wk,src)
            A[blk(k),(k+1)*BS:]=P
            for i in range(k+1,nblk):
                o=(i-k-1)*BS
                old=k_ref[0,blk(i),i*BS:].astype(jnp.float32) if k==0 else A[blk(i),i*BS:]
                A[blk(i),i*BS:]=old-dotT(P[:,o:o+BS],P[:,o:])
        rhs=jnp.where(keep(k),c_ref[0,blk(k),:].astype(jnp.float32),0.0)
        if k>0: rhs=rhs-dotT(A[0:k*BS,blk(k)],Z[0:k*BS,:])
        Z[blk(k),:]=dot(Wk,rhs)
    for k in reversed(range(nblk)):
        z=Z[blk(k),:]
        if k<nblk-1: z=z-dot(A[blk(k),(k+1)*BS:],Z[(k+1)*BS:,:])
        x=dotT(W[k],z)
        Z[blk(k),:]=x
        x_ref[blk(k),:]=jnp.where(keep(k),x,0.0).astype(jnp.bfloat16)
def scen_solve(kkt,coupling,active,cols):
    n=kkt.shape[1]
    return pl.pallas_call(scen_kernel,
        out_shape=jax.ShapeDtypeStruct((n,cols),jnp.bfloat16),
        in_specs=[pl.BlockSpec(memory_space=pltpu.SMEM),pl.BlockSpec((1,n,n),lambda i:(0,0,0)),pl.BlockSpec((1,n,cols),lambda i:(0,0,0))],
        out_specs=pl.BlockSpec((n,cols),lambda i:(0,0)),
        grid=(1,),
        scratch_shapes=[pltpu.VMEM((n,n),jnp.float32),pltpu.VMEM((n,cols),jnp.float32),pltpu.VMEM((n//BS,BS,BS),jnp.float32)],
        compiler_params=pltpu.CompilerParams(vmem_limit_bytes=48*2**20),
        name="scen_solve")(active,kkt,coupling)
def pivot_kernel(s_ref,w_ref,A):
    n=s_ref.shape[0]; nblk=n//BS
    blk=lambda k: slice(k*BS,(k+1)*BS)
    for k in range(nblk):
        _,Wk=base128(s_ref[blk(k),blk(k)] if k==0 else A[blk(k),blk(k)])
        if k<nblk-1:
            P=dot(Wk,s_ref[blk(k),(k+1)*BS:] if k==0 else A[blk(k),(k+1)*BS:])
            A[blk(k),(k+1)*BS:]=P
            for i in range(k+1,nblk):
                o=(i-k-1)*BS
                old=s_ref[blk(i),i*BS:] if k==0 else A[blk(i),i*BS:]
                A[blk(i),i*BS:]=old-dotT(P[:,o:o+BS],P[:,o:])
            w_ref[blk(k),(k+1)*BS:]=jnp.zeros((BS,n-(k+1)*BS),jnp.float32)
        w_ref[blk(k),blk(k)]=Wk
        if k>0:
            w_ref[blk(k),0:k*BS]=-dot(Wk,dotT(A[0:k*BS,blk(k)],w_ref[0:k*BS,0:k*BS]))
def pivot_inv(s):
    n=s.shape[0]
    return pl.pallas_call(pivot_kernel,out_shape=jax.ShapeDtypeStruct((n,n),jnp.float32),
        scratch_shapes=[pltpu.VMEM((n,n),jnp.float32)],
        compiler_params=pltpu.CompilerParams(vmem_limit_bytes=32*2**20),name="pivot_inv")(s)


PW = 256


def per_device(coupling, scen_kkt, active_rows, first_hess):
    _, _, coupled = coupling.shape
    own_rows = coupled // lax.axis_size("scen")
    scen_idx = lax.axis_index("scen")
    panel_cols = 2 * PW
    solved = scen_solve(scen_kkt, coupling, active_rows, panel_cols)
    pivot = dotT(coupling[0, :, :panel_cols], solved, None)
    pivot = lax.psum(pivot, ("scen", "grp")) + jnp.diag(first_hess)
    own_panel = lax.psum_scatter(
        dotT(coupling[0], solved, None), "scen", scatter_dimension=0, tiled=True
    )
    own_panel = lax.psum(own_panel, "grp")
    global_row = scen_idx * own_rows + lax.broadcasted_iota(jnp.int32, (own_rows, 1), 0)
    col_ids = lax.broadcasted_iota(jnp.int32, (1, panel_cols), 1)
    own_panel = own_panel + jnp.where(global_row == col_ids, first_hess[None, :], 0.0)
    inv = pivot_inv(pivot)
    rows = lax.dot_general(
        own_panel, inv, (((1,), (1,)), ((), ())), precision=H, preferred_element_type=jnp.float32
    )
    return jnp.where(global_row < col_ids, 0.0, rows)


def solution(mesh):
    placed = (
        P(("scen", "grp"), None, None),
        P(("scen", "grp"), None, None),
        P(("scen", "grp")),
        P(),
    )
    return jax.shard_map(
        per_device, mesh=mesh, in_specs=placed, out_specs=P("scen", None), check_vma=False
    )
```

time: 586 us -> 279 us (0.48); the launches traced: 576 us -> 276 us
  other arithmetic: 301 us -> 1.38 us
  Pallas kernels: 0 us -> 64.4 us
  local copies, waits for them, and re-layouts: 35.4 us -> 1.27 us
  matrix products: 33.7 us -> 12.6 us
    another operation x44 -> x0, other arithmetic: 294 us -> none  [the longest x22 124 us: per_device(): factor = jnp.linalg.cholesky(scen_kkt.astype(jnp.float32))]
    pallas_call x0 -> x2, Pallas kernels: none -> 64.4 us  [the longest x1 46.4 us: scen_solve(): pl.pallas_call(scen_kernel, out_shape=jax.ShapeDtypeStruct((n, cols), jnp...]
    another operation x51 -> x0, local copies, waits for them, and re-layouts: 30.1 us -> none
    another operation x45 -> x0, matrix products: 25.5 us -> none  [the longest x22 11 us: solve_block(): return jax.scipy.linalg.cho_solve((factor, True), right_side)]
    psum x1, waiting for transfers between devices: 54.1 us -> 33.6 us  [per_device(): own_panel = lax.psum(own_panel, 'grp')]
    psum x1, waiting for transfers between devices: 56.5 us -> 74.7 us  [per_device(): pivot = lax.psum(pivot, ('scen', 'grp')) + jnp.diag(first_hess)]
  transfers between devices with their start and end apart: 3 -> 3, of which waited for: 3 -> 3; matrix products, arithmetic and copies ran while one was open for 0% -> 1% of each run, Pallas kernels for 0% -> 6%
where the time goes in v1:
time: 279 us; the launch traced here: 276 us
  waiting for transfers between devices  180 us (65%)
  Pallas kernels  64.4 us (23%)
  between operations  15.8 us (6%)
  matrix products  12.6 us (5%)
    psum x1, waiting for transfers between devices, per_device(): pivot = lax.psum(pivot, ('scen', 'grp')) + jnp.diag(first_hess)  74.7 us
    reduce_scatter x1, waiting for transfers between devices, per_device(): lax.psum_scatter(dotT(coupling[0], solved, None), 'scen', scatter_dimensi...  72.1 us
    pallas_call x1, Pallas kernels, scen_solve(): pl.pallas_call(scen_kernel, out_shape=jax.ShapeDtypeStruct((n, cols), jnp...  46.4 us
    psum x1, waiting for transfers between devices, per_device(): own_panel = lax.psum(own_panel, 'grp')  33.6 us
    pallas_call x1, Pallas kernels, pivot_inv(): pl.pallas_call(pivot_kernel, out_shape=jax.ShapeDtypeStruct((n, n), jnp.f...  17.9 us
    dot_general x2, matrix products, dotT(): lax.dot_general(a, b, (((0,), (0,)), ((), ())), precision=prec, preferred...  8.41 us
  transfers between devices with their start and end apart: 3, of which 3 were waited for; matrix products, arithmetic and copies ran while one was open for 1% of the time, Pallas kernels for 6%

profile of v1, /device:TPU:0, one launch (start us, length us, event | category | flops | bytes accessed | tf_op | source)
XLA Modules:
  0.0 275.9 jit_solution(3990584991747999074)
XLA Ops:
  7.4 0.0 reduce-scatter.2.cloned.1.call-start
  8.0 0.0 copy-start
  8.0 1.3 copy-done
  9.3 0.0 copy-start.1
  9.3 46.4 %scen_solve.1 = bf16[768,512]{1,0:T(8,128)(2,1)S(1)} custom-call(s32[1]{0:T(128)S(6)} %copy.7.act_ref, bf16[1,768,768]{2,1,0:T(8,128)(2,1)S(1)} %copy-done, bf16[1,768,4096]{2,1,0:T(8,128)(2,1)} %c_ref.1), custom_call_target="tpu_custom_call" | custom-call | tf_op jit(solution)/shard_map/scen_solve/pallas_call | solution.py:93
  55.7 0.0 copy-done.1
  55.8 5.7 %convolution_bitcast_fusion = f32[4096,512]{1,0:T(8,128)} fusion(bf16[768,512]{1,0:T(8,128)(2,1)S(1)} %scen_solve.1, bf16[1,768,4096]{2,1,0:T(8,128)(2,1)S(1)} %copy-done.1), kind=kOutput, calls=%fused_computation | convolution fusion | flops 3221225472 | bytes 15466496 | tf_op jit(solution)/shard_map/dot_general | solution.py:60
  61.4 0.0 copy-start.2
  61.4 0.0 reduce-scatter.2.cloned.1.call-update
  61.5 0.0 all-reduce.5.cloned.1.call-start
  61.5 2.7 convolution_bitcast_fusion.1
  64.2 0.0 all-reduce.5.cloned.1.call-update
  64.3 0.0 all-reduce.3.cloned.1.call-start
  64.3 72.1 %reduce-scatter.2.cloned.1.call-done = f32[512,512]{1,0:T(8,128)} async-done(((f32[4096,512]{1,0:T(8,128)}), f32[512,512]{1,0:T(8,128)}) %reduce-scatter.2.cloned.1.call-update) | async-done | bytes 1048592 | tf_op jit(solution)/shard_map/reduce_scatter | solution.py:135
  136.4 0.0 all-reduce.3.cloned.1.call-update
  136.5 74.7 %all-reduce.5.cloned.1.call-done = f32[512,512]{1,0:T(8,128)} async-done(((f32[512,512]{1,0:T(8,128)}), f32[512,512]{1,0:T(8,128)}) %all-reduce.5.cloned.1.call-update) | async-done | bytes 1048592 | tf_op jit(solution)/shard_map/psum | solution.py:134
  211.2 0.0 copy-done.2
  211.2 1.4 select_add_fusion.s_ref
  212.6 17.9 %pivot_inv.1 = f32[512,512]{1,0:T(8,128)S(1)} custom-call(f32[512,512]{1,0:T(8,128)S(1)} %select_add_fusion.s_ref), custom_call_target="tpu_custom_call" | custom-call | tf_op jit(solution)/shard_map/pivot_inv/pallas_call | solution.py:119
  230.5 33.6 %all-reduce.3.cloned.1.call-done = f32[512,512]{1,0:T(8,128)} async-done(((f32[512,512]{1,0:T(8,128)}), f32[512,512]{1,0:T(8,128)}) %all-reduce.3.cloned.1.call-update) | async-done | bytes 1048592 | tf_op jit(solution)/shard_map/psum | solution.py:138
  264.1 4.2 %convolution_select_fusion = f32[512,512]{1,0:T(8,128)} fusion(f32[512,512]{1,0:T(8,128)S(1)} %pivot_inv.1, f32[512,512]{1,0:T(8,128)} %all-reduce.3.cloned.1.call-done, f32[512]{0:T(512)S(1)} %copy-done.2, s32[512]{0:T(512)S(1)} %iota_add_fusion), kind=kOutput, calls=%fused_computation.2 | convolution fusion | flops 1611923456 | bytes 3149824 | tf_op jit(solution)/shard_map/dot_general | solution.py:143
  (1 shorter events, 0.0 us)
Async XLA Ops:
  7.4 129.0 %reduce-scatter.2.cloned.1.call-start = ((), (), s32[]{:S(2)}) async-start(), calls=%async_computation.1 | async-start | bytes 9437184 | tf_op jit(solution)/shard_map/reduce_scatter | solution.py:135
  8.0 1.3 copy-start
  9.3 46.5 %copy-start.1 = (bf16[1,768,4096]{2,1,0:T(8,128)(2,1)S(1)}, bf16[1,768,4096]{2,1,0:T(8,128)(2,1)}, u32[]{:S(2)}) copy-start(bf16[1,768,4096]{2,1,0:T(8,128)(2,1)} %c_ref.1) | copy-start | bytes 18874372
  61.4 149.7 %copy-start.2 = (f32[512]{0:T(512)S(1)}, f32[512]{0:T(512)}, u32[]{:S(2)}) copy-start(f32[512]{0:T(512)} %param.7) | copy-start | bytes 6148
  61.5 149.7 %all-reduce.5.cloned.1.call-start = ((), (), s32[]{:S(2)}) async-start(), calls=%async_computation.3 | async-start | bytes 2097152 | tf_op jit(solution)/shard_map/psum | solution.py:134
  64.3 199.8 %all-reduce.3.cloned.1.call-start = ((), (), s32[]{:S(2)}) async-start(), calls=%async_computation.2 | async-start | bytes 2097152 | tf_op jit(solution)/shard_map/psum | solution.py:138
Sparse Core Ops, SparseCore 0:
  61.6 74.7 reduce-scatter.1
Sparse Core Ops, SparseCore 1:
  67.1 144.0 all-reduce.4
  213.4 50.6 all-reduce.2

commit v2 on v1

v2 whole, which is shorter than its diff:
```python
import jax
import jax.numpy as jnp
from jax import lax
from jax.experimental import pallas as pl
from jax.experimental.pallas import tpu as pltpu
from jax.sharding import PartitionSpec as P

H=lax.Precision.HIGHEST
def bc(x,s): return jnp.broadcast_to(x[s:s+1,:], x.shape)
def halves(x):
    hi=x.astype(jnp.bfloat16)
    return hi,(x-hi.astype(jnp.float32)).astype(jnp.bfloat16)
def dot3(a,b,dims):
    (i,),(j,)=dims
    ah,al=halves(a); bh,bl=halves(b)
    return lax.dot_general(jnp.concatenate([ah,ah,al],i),jnp.concatenate([bh,bl,bh],j),(dims,((),())),preferred_element_type=jnp.float32)
def elim(R, off, nb):
    ng=nb//8; nh=len(R[0])
    row=lax.broadcasted_iota(jnp.int32,(8,128),0)
    L={}
    for j in range(nb):
        for g in range(j//8,ng):
            L[j,g]=jnp.broadcast_to(R[g][0][:,off+j:off+j+1],(8,128))
    out=[None]*ng
    a=bc(L[0,0],0); b=bc(L[0,0],1); c=bc(L[1,0],1)
    for j in range(0,nb,2):
        gj=j//8; s=j%8
        det=a*c-b*b
        rd=1.0/det
        al={}; be={}
        for g in range(gj,ng):
            x=L[j,g]*c-L[j+1,g]*b; y=L[j+1,g]*a-L[j,g]*b
            if g==gj:
                x=jnp.where(row>s+1,x,0.0); y=jnp.where(row>s+1,y,0.0)
            al[g]=x; be[g]=y
        nxt=None
        if j+2<nb:
            k=j+2; g=k//8; t=k%8
            p,q,p2,q2=bc(L[j,g],t),bc(L[j+1,g],t),bc(L[j,g],t+1),bc(L[j+1,g],t+1)
            x,y,x2,y2=bc(al[g],t),bc(be[g],t),bc(al[g],t+1),bc(be[g],t+1)
            nxt=(bc(L[k,g],t)-(x*p+y*q)*rd, bc(L[k,g],t+1)-(x2*p+y2*q)*rd, bc(L[k+1,g],t+1)-(x2*p2+y2*q2)*rd)
        for k in range(j+2,nb):
            p=bc(L[j,k//8],k%8); q=bc(L[j+1,k//8],k%8)
            for g in range(k//8,ng):
                L[k,g]=L[k,g]-(al[g]*p+be[g]*q)*rd
        r1=[bc(R[gj][h],s) for h in range(nh)]; r2=[bc(R[gj][h],s+1) for h in range(nh)]
        ra=1.0/a
        sa=lax.rsqrt(a); sb=lax.rsqrt(det*ra); ba=b*ra
        if s==0: out[gj]=[jnp.zeros((8,128),jnp.float32)]*nh
        for h in range(nh):
            out[gj][h]=jnp.where(row==s,r1[h]*sa,jnp.where(row==s+1,(r2[h]-ba*r1[h])*sb,out[gj][h]))
        for g in range(gj,ng):
            if g==gj and s==6: continue
            x=al[g]*rd; y=be[g]*rd
            R[g]=[R[g][h]-(x*r1[h]+y*r2[h]) for h in range(nh)]
        if nxt: a,b,c=nxt
    return out
def base128(A, exact=False, nb=32, between=None):
    row=lax.broadcasted_iota(jnp.int32,(8,128),0); lane=lax.broadcasted_iota(jnp.int32,(8,128),1)
    M=[[A[8*g:8*g+8,:],jnp.where(lane==row+8*g,1.0,0.0)] for g in range(16)]
    outs=[]
    n=128//nb; ng=nb//8
    for c in range(n):
        if between: between[c]()
        o=elim(M[c*ng:(c+1)*ng],c*nb,nb)
        outs+=o
        if c<n-1:
            O=[jnp.concatenate([o[g][h] for g in range(ng)],0) for h in range(2)]
            O2=jnp.concatenate(O,1)
            dims=((0,),(0,))
            if exact: T=lax.dot_general(O[0],O2,(dims,((),())),precision=H,preferred_element_type=jnp.float32)
            else: T=dot3(O[0],O2,dims)
            for g in range((c+1)*ng,16):
                M[g]=[M[g][h]-T[8*g:8*g+8,128*h:128*h+128] for h in range(2)]
    return [jnp.concatenate([outs[g][h] for g in range(16)],0) for h in range(2)]
BS=128
def dotT(a,b,prec=H): return lax.dot_general(a,b,(((0,),(0,)),((),())),precision=prec,preferred_element_type=jnp.float32)
def dot(a,b,prec=H): return lax.dot_general(a,b,(((1,),(0,)),((),())),precision=prec,preferred_element_type=jnp.float32)
def scen_kernel(act_ref,k_ref,c_hbm,x_ref,M,D,Wk,left,right,row_ref,inv_ref,panel_ref,sem):
    n=k_ref.shape[1]; nblk=n//BS
    fetch=pltpu.make_async_copy(c_hbm.at[0,:,0:panel_ref.shape[1]],panel_ref,sem)
    fetch.start()
    M[...]=k_ref[0].astype(jnp.float32)
    D[...]=k_ref[0,0:BS,0:BS].astype(jnp.float32)
    Wk[...]=jnp.zeros_like(Wk)
    eye=jnp.where(lax.broadcasted_iota(jnp.int32,(BS,BS),0)==lax.broadcasted_iota(jnp.int32,(BS,BS),1),1.0,0.0)
    def sweep(k,live):
        here=pl.ds(pl.multiple_of(k*BS,BS),BS)
        def invert():
            W=Wk[...]
            inv_ref[...]=dotT(W,W)
            col_hi,col_lo=halves(jnp.where(live,M[:,here],0.0))
            left[:,0:BS]=col_hi; left[:,BS:2*BS]=col_hi; left[:,2*BS:]=col_lo
            left[here,:]=jnp.zeros((BS,3*BS),jnp.bfloat16)
        def scale():
            inv=inv_ref[...]
            row=dot3(inv,M[here,:],((1,),(0,)))
            row_ref[...]=row
            row_ref[:,here]=eye-inv
            hi,lo=halves(row_ref[...])
            right[0:BS,:]=hi; right[BS:2*BS,:]=lo; right[2*BS:,:]=hi
            row_ref[...]=row
            row_ref[:,here]=-inv
        def spread(rows):
            M[rows,:]=M[rows,:]-dot(left[rows,:],right[...],None)
        def first(): spread(slice(0,n//2))
        def second():
            spread(slice(n//2,n))
            M[here,:]=jnp.where(live,row_ref[...],M[here,:])
        return invert,scale,first,second
    def step(k,_):
        here=pl.ds(pl.multiple_of(k*BS,BS),BS)
        follow=pl.ds(pl.multiple_of(jnp.minimum(k+1,nblk-1)*BS,BS),BS)
        _,W=base128(D[...],between=sweep(jnp.maximum(k-1,0),k>0))
        P=dot3(W,M[here,follow],((1,),(0,)))
        D[...]=M[follow,follow]-dot3(P,P,((0,),(0,)))
        Wk[...]=W
        return 0
    lax.fori_loop(0,nblk,step,0)
    for part in sweep(nblk-1,True): part()
    fetch.wait()
    kept=lax.broadcasted_iota(jnp.int32,(n,1),0)<act_ref[0]
    panel=jnp.where(kept,panel_ref[...],jnp.zeros((),jnp.bfloat16))
    hi,lo=halves(M[...])
    x=dotT(panel,hi,None)+dotT(panel,lo,None)
    kept=lax.broadcasted_iota(jnp.int32,(1,n),1)<act_ref[0]
    x_ref[...]=jnp.where(kept,-x,0.0).astype(jnp.bfloat16)
def scen_solve(kkt,coupling,active,cols):
    n=kkt.shape[1]
    vm=pltpu.VMEM
    return pl.pallas_call(scen_kernel,
        out_shape=jax.ShapeDtypeStruct((cols,n),jnp.bfloat16),
        in_specs=[pl.BlockSpec(memory_space=pltpu.SMEM),pl.BlockSpec(memory_space=vm),pl.BlockSpec(memory_space=pl.ANY)],
        out_specs=pl.BlockSpec(memory_space=vm),
        scratch_shapes=[vm((n,n),jnp.float32),vm((BS,BS),jnp.float32),vm((BS,BS),jnp.float32),vm((n,3*BS),jnp.bfloat16),
            vm((3*BS,n),jnp.bfloat16),vm((BS,n),jnp.float32),vm((BS,BS),jnp.float32),vm((n,cols),jnp.bfloat16),pltpu.SemaphoreType.DMA],
        compiler_params=pltpu.CompilerParams(vmem_limit_bytes=48*2**20),
        name="scen_solve")(active,kkt,coupling)
def blk(k): return slice(k*BS,(k+1)*BS)
def sym(a): return 0.5*(a+a.T)
def upper_blocks(m): return [(i,j) for i in range(m) for j in range(i,m)]
def packed_places(m):
    places,slots={},[]
    blocks=upper_blocks(m)
    full=len(blocks)//m*m
    for q,ij in enumerate(blocks[:full]): places[ij]=[(0,q//m*BS,q%m,BS)]
    rest=blocks[full:]
    cut=BS*len(rest)//m
    for q,ij in enumerate(rest):
        per=BS//cut
        places[ij]=[(t*cut,full//m*BS,q*per+t,cut) for t in range(per)]
    return places,full//m*BS+(cut if rest else 0)
def lanes(g): return slice(g*BS,(g+1)*BS)
def pivot_prod_kernel(xt_ref,c_ref,o_ref):
    n=xt_ref.shape[0]; half=n//2; per=half//BS
    T=dot(xt_ref[...],c_ref[0],None)
    D=[sym(T[:half,:half]),sym(T[half:,half:])]
    for (i,j),where in packed_places(n//BS)[0].items():
        if i//per==j//per: v=D[i//per][blk(i%per),blk(j%per)]
        else: v=T[blk(i),blk(j)]
        for r,row,g,rows in where: o_ref[row:row+rows,lanes(g)]=v[r:r+rows,:]
def pivot_prod(xt,coupling):
    cols,n=xt.shape
    high=packed_places(cols//BS)[1]
    return pl.pallas_call(pivot_prod_kernel,
        out_shape=jax.ShapeDtypeStruct((high,cols),jnp.float32),grid=(1,),
        in_specs=[pl.BlockSpec((cols,n),lambda i:(0,0)),pl.BlockSpec((1,n,cols),lambda i:(0,0,0))],
        out_specs=pl.BlockSpec((high,cols),lambda i:(0,0)),
        compiler_params=pltpu.CompilerParams(vmem_limit_bytes=48*2**20),
        cost_estimate=pl.CostEstimate(flops=2*cols*cols*n,bytes_accessed=4*cols*n+4*high*cols,transcendentals=0),
        name="pivot_prod")(xt,coupling)
def panel_factor(A,wt_ref,l_ref,base):
    n=A.shape[1]; end=base+2*BS
    eye=lax.broadcasted_iota(jnp.int32,(BS,BS),0)<=lax.broadcasted_iota(jnp.int32,(BS,BS),1)
    WT=[]
    for k in range(2):
        lo=base+k*BS; me=slice(lo,lo+BS)
        Uk,Wk=base128(A[me,me])
        WT.append(Wk.T)
        l_ref[lo-base:lo-base+BS,blk(k)]=jnp.where(eye,Uk,0.0).T
        if lo+BS<n:
            P=dot3(Wk,A[me,lo+BS:],((1,),(0,)))
            A[me,lo+BS:]=P
            for i in range((n-lo)//BS-1):
                r=lo+(i+1)*BS
                if r<end: A[r:r+BS,r:]=A[r:r+BS,r:]-dot3(P[:,i*BS:(i+1)*BS],P[:,i*BS:],((0,),(0,)))
                l_ref[r-base:r-base+BS,blk(k)]=P[:,i*BS:(i+1)*BS].T
    l_ref[0:BS,blk(1)]=jnp.zeros((BS,BS),jnp.float32)
    top=wt_ref.shape[0]-2*BS
    wt_ref[top:top+BS,blk(0)]=WT[0]
    wt_ref[top+BS:,blk(0)]=jnp.zeros((BS,BS),jnp.float32)
    wt_ref[top:top+BS,blk(1)]=-dot(dot(WT[0],A[base:base+BS,base+BS:end]),WT[1])
    wt_ref[top+BS:,blk(1)]=WT[1]
def pivot_one_kernel(perm_ref,hess_ref,*refs):
    srcs,(wt_ref,l_ref,u_ref,rest_ref,A,pk)=refs[:-6],refs[-6:]
    n=A.shape[0]; nblk=n//BS; half=n//2
    each=perm_ref.shape[0]//len(srcs)
    rows=srcs[0].shape[0]//each
    for s,src in enumerate(srcs):
        for q in range(each):
            dst=pl.multiple_of(perm_ref[s*each+q]*rows,8)
            pk[pl.ds(dst,rows),:]=src[q*rows:(q+1)*rows,:]
    diag=lax.broadcasted_iota(jnp.int32,(BS,BS),0)==lax.broadcasted_iota(jnp.int32,(BS,BS),1)
    for (i,j),where in packed_places(nblk)[0].items():
        parts=[pk[row:row+high,lanes(g)] for _,row,g,high in where]
        v=parts[0] if len(parts)==1 else jnp.concatenate(parts,0)
        A[blk(i),blk(j)]=v+jnp.where(diag,hess_ref[:,blk(i)],0.0) if i==j else v
    panel_factor(A,wt_ref,l_ref,0)
    u=A[0:half,half:]
    u_ref[...]=u
    for k in range(half//BS):
        o=k*BS
        rest_ref[o:o+BS,o:]=A[half+o:half+o+BS,half+o:]-dot3(u[:,o:o+BS],u[:,o:],((0,),(0,)))
    rest_ref[BS:,0:BS]=jnp.zeros((BS,BS),jnp.float32)
def pivot_one(perm,hess,*srcs):
    n=hess.shape[0]; total=sum(s.shape[0] for s in srcs)
    sd=lambda r,c: jax.ShapeDtypeStruct((r,c),jnp.float32)
    vm=pl.BlockSpec(memory_space=pltpu.VMEM)
    return pl.pallas_call(pivot_one_kernel,out_shape=[sd(n//2,n//2),sd(n,n//2),sd(n//2,n//2),sd(n//2,n//2)],
        in_specs=[pl.BlockSpec(memory_space=pltpu.SMEM)]+[vm]*(1+len(srcs)),out_specs=[vm]*4,
        scratch_shapes=[pltpu.VMEM((n,n),jnp.float32),pltpu.VMEM((total,n),jnp.float32)],
        cost_estimate=pl.CostEstimate(flops=10**10,bytes_accessed=4*2**20,transcendentals=0),
        compiler_params=pltpu.CompilerParams(vmem_limit_bytes=16*2**20),name="pivot_one")(perm,hess[None],*srcs)
def pivot_two_kernel(wt1_ref,u_ref,rest_ref,wt_ref,l_ref,A):
    half=wt1_ref.shape[0]
    A[...]=rest_ref[...]
    panel_factor(A,wt_ref,l_ref,0)
    wt_ref[0:half,:]=-dot(wt1_ref[...],dot(u_ref[...],wt_ref[half:,:]))
def pivot_two(wt1,u,rest):
    half=wt1.shape[0]
    sd=lambda r,c: jax.ShapeDtypeStruct((r,c),jnp.float32)
    vm=pl.BlockSpec(memory_space=pltpu.VMEM)
    return pl.pallas_call(pivot_two_kernel,out_shape=[sd(2*half,half),sd(half,half)],
        in_specs=[vm]*3,out_specs=[vm]*2,scratch_shapes=[pltpu.VMEM((half,half),jnp.float32)],
        cost_estimate=pl.CostEstimate(flops=10**10,bytes_accessed=4*2**20,transcendentals=0),
        compiler_params=pltpu.CompilerParams(vmem_limit_bytes=16*2**20),name="pivot_two")(wt1,u,rest)


PW = 256
HALF = 256
CUTS = (0, 72, 168, 256)
UNIT = 40
FIRST = 24
HOPS = {"x": ("scen", 2), "y": ("scen", 4), "z": ("grp", 1)}
ORDERS = ("xyz", "yzx", "zxy")


def flip(array, axis, mask):
    size = lax.axis_size(axis)
    return lax.ppermute(array, axis, [(i, i ^ mask) for i in range(size)])


def after(array, *others):
    return lax.optimization_barrier((array,) + others)[0]


def products_kernel(where_ref, xt_ref, c_ref, packed_ref, a_ref, b_ref, z_ref):
    slab = where_ref[pl.program_id(0)]
    total = dot(xt_ref[...], c_ref[0], None)
    for half in range(2):
        z = where_ref[4] ^ half
        part = total[half * HALF : (half + 1) * HALF, :]
        a_ref[pl.ds(z, 1), : CUTS[1], :] = part[CUTS[0] : CUTS[1], :][None]
        b_ref[0, pl.ds(z, 1), 0] = part[CUTS[1] : CUTS[2], :][None]
        z_ref[pl.ds(z, 1), 0] = part[CUTS[2] : CUTS[3], :][None]
    unit = pl.multiple_of(slab * UNIT, 8)
    a_ref[0, CUTS[1] :, :] = packed_ref[pl.ds(unit, FIRST), :]
    rest = UNIT - FIRST
    a_ref[1, CUTS[1] : CUTS[1] + rest, :] = packed_ref[pl.ds(unit + FIRST, rest), :]
    a_ref[1, CUTS[1] + rest :, :] = jnp.zeros((FIRST - rest, a_ref.shape[2]), jnp.float32)


def panel_products(where, xt, coupling, packed):
    cols, rows = xt.shape
    own = coupling.shape[2] // 8
    high = [CUTS[1] + FIRST, CUTS[2] - CUTS[1], CUTS[3] - CUTS[2]]
    shapes = [(8, high[0], own), (2, 2, 2, high[1], own), (2, 4, high[2], own)]
    pieces = pl.pallas_call(
        products_kernel,
        out_shape=[jax.ShapeDtypeStruct(shape, jnp.float32) for shape in shapes],
        grid_spec=pltpu.PrefetchScalarGridSpec(
            num_scalar_prefetch=1,
            grid=(4,),
            in_specs=[
                pl.BlockSpec((cols, rows), lambda s, w: (0, 0)),
                pl.BlockSpec((1, rows, own), lambda s, w: (0, 0, w[s])),
                pl.BlockSpec(packed.shape, lambda s, w: (0, 0)),
            ],
            out_specs=[
                pl.BlockSpec((2, high[0], own), lambda s, w: (s, 0, 0)),
                pl.BlockSpec((1, 2, 1, high[1], own), lambda s, w: (s % 2, 0, s // 2, 0, 0)),
                pl.BlockSpec((2, 1, high[2], own), lambda s, w: (0, s, 0, 0)),
            ],
        ),
        cost_estimate=pl.CostEstimate(
            flops=8 * own * cols * rows, bytes_accessed=8 * own * (rows + 4 * cols), transcendentals=0
        ),
        compiler_params=pltpu.CompilerParams(vmem_limit_bytes=56 * 2**20),
        name="panel_products",
    )(where, xt, coupling, packed)
    return [p.reshape((8,) + p.shape[-2:]) for p in pieces]


def final_kernel(where_ref, wt1_ref, wt2_ref, l1_ref, l2_ref, mine_ref, other_ref, *refs, part):
    out_ref = refs[-1]

    @pl.when(where_ref[1] == 0)
    def _():
        out_ref[:, :PW] = l1_ref[part * HALF : (part + 1) * HALF, :]
        out_ref[:, PW:] = l2_ref[...] if part else jnp.zeros_like(l2_ref)

    @pl.when(where_ref[1] > 0)
    def _():
        swap = where_ref[0] > 0
        one = jnp.where(swap, other_ref[...], mine_ref[...])
        two = jnp.where(swap, mine_ref[...], other_ref[...])
        out_ref[:, :PW] = dotT(one, wt1_ref[...])
        out_ref[:, PW:] = dotT(one, wt2_ref[:PW, :]) + dotT(two, wt2_ref[PW:, :])


def final_rows(where, inverse, mine, other, part, held=None):
    vmem = pl.BlockSpec(memory_space=pltpu.VMEM)
    block = lambda *shape: pl.BlockSpec(shape, lambda i: (0, 0))
    args = (where, *inverse, mine, other) + (() if held is None else (held,))
    return pl.pallas_call(
        lambda *refs: final_kernel(*refs, part=part),
        out_shape=jax.ShapeDtypeStruct((2 * HALF, 2 * PW), jnp.float32),
        grid=(1,),
        in_specs=[pl.BlockSpec(memory_space=pltpu.SMEM)]
        + [block(*a.shape) for a in args[1:7]]
        + [pl.BlockSpec(memory_space=pl.ANY)] * (held is not None),
        out_specs=pl.BlockSpec((HALF, 2 * PW), lambda i: (part, 0)),
        input_output_aliases={} if held is None else {7: 0},
        compiler_params=pltpu.CompilerParams(vmem_limit_bytes=16 * 2**20),
        name="owned_rows",
    )(*args)


def on_slice(coupling, scen_kkt, active_rows, first_hess):
    panel_cols = 2 * PW
    scen_idx = lax.axis_index("scen")
    core, spot = scen_idx % 2, scen_idx // 2
    side = lax.axis_index("grp") % 2

    def where_of(core_bit):
        slabs = [scen_idx ^ (y * 4 + x * 2 + core_bit) for x in range(2) for y in range(2)]
        return jnp.stack(slabs + [side]).astype(jnp.int32)

    wheres = [where_of(0), where_of(1)]
    perm = jnp.stack([(spot ^ m) * 2 + (core ^ c) for c in range(2) for m in range(4)])
    perm = perm.astype(jnp.int32)
    scen_kkt = after(scen_kkt, *wheres, perm)
    xt = scen_solve(scen_kkt, coupling, active_rows, panel_cols)

    packed = pivot_prod(xt, coupling)
    away = panel_products(wheres[1], xt, coupling, packed)
    got = [flip(piece, "scen", 1) for piece in away]
    keeps = panel_products(wheres[0], after(xt, *away), coupling, packed)

    sends, token = [], []
    for i in range(3):
        sends.append(keeps[i][4:] + after(got[i], *token)[4:])
        token = [sends[i]]
    fresh = [flip(sends[i], *HOPS[ORDERS[i][0]]) for i in range(3)]
    keeps = [keeps[i][:4] + after(got[i], *sends)[:4] for i in range(3)]
    got = fresh
    got[0] = after(got[0], *keeps)
    sends, token = [], []
    for i in range(3):
        sends.append(keeps[i][2:] + after(got[i], *token)[2:])
        token = [sends[i]]
    fresh = [flip(sends[i], *HOPS[ORDERS[i][1]]) for i in range(3)]
    keeps = [keeps[i][:2] + after(got[i], *sends)[:2] for i in range(3)]
    got = fresh
    got[0] = after(got[0], *keeps)
    main = CUTS[1]
    unit = jnp.concatenate(
        [
            keeps[0][0, main:] + got[0][0, main:],
            keeps[0][1, main : main + UNIT - FIRST] + got[0][1, main : main + UNIT - FIRST],
        ],
        0,
    )
    keeps[0], got[0] = keeps[0][:, :main], got[0][:, :main]
    sends, token = [], []
    for i in range(3):
        sends.append(keeps[i][1:] + after(got[i], *token)[1:])
        token = [sends[0], unit]
    fresh = [flip(sends[i], *HOPS[ORDERS[i][2]]) for i in range(3)]
    over_z = flip(unit, "grp", 1)
    keeps = [keeps[i][:1] + after(got[i], *sends)[:1] for i in range(3)]
    unit = unit + after(over_z, *keeps)
    over_z = flip(unit, "grp", 2)
    fresh = [after(f, unit) for f in fresh]
    slab = jnp.concatenate([keeps[i][0] + fresh[i][0] for i in range(3)], 0)
    parts = [slab[:, part * HALF : (part + 1) * HALF] for part in range(2)]
    unit = unit + after(over_z, *parts)
    rest = [unit] + [flip(unit, "scen", 2 * mask) for mask in (1, 2, 3)]

    got_one = flip(parts[0], "grp", 2)
    pivot_half = jnp.concatenate(rest, 0)
    pivot_other = flip(pivot_half, "scen", 1)
    one = parts[0] + after(got_one, pivot_half)
    one_other = flip(one, "grp", 1)
    got_two = flip(after(parts[1], one), "grp", 2)
    wt1, l1, u, left = pivot_one(perm, first_hess, after(pivot_half, one), pivot_other)
    wt2, l2 = pivot_two(wt1, u, left)
    two = parts[1] + after(got_two, left)
    two_other = flip(two, "grp", 1)
    where = jnp.stack([side, scen_idx]).astype(jnp.int32)
    inverse = (wt1, wt2, l1, l2)
    rows = final_rows(where, inverse, one, after(one_other, two, wt2), 0)
    return final_rows(where, inverse, two, after(two_other, rows), 1, rows)


def any_mesh(coupling, scen_kkt, active_rows, first_hess):
    panel_cols = 2 * PW
    own_rows = coupling.shape[2] // lax.axis_size("scen")
    start = lax.axis_index("scen") * own_rows
    xt = scen_solve(scen_kkt, coupling, active_rows, panel_cols)
    packed = lax.psum(pivot_prod(xt, coupling), ("scen", "grp"))
    wt1, l1, u, left = pivot_one(jnp.zeros((1,), jnp.int32), first_hess, packed)
    wt2, l2 = pivot_two(wt1, u, left)
    own = lax.psum_scatter(
        dot(xt, coupling[0], None), "scen", scatter_dimension=1, tiled=True
    )
    own = lax.psum(own, "grp")
    rows = jnp.concatenate([dotT(own[:PW], wt1), dotT(own, wt2)], 1)
    factor = jnp.concatenate([l1, jnp.concatenate([jnp.zeros_like(l2), l2], 0)], 1)
    padded = jnp.concatenate([factor, jnp.zeros((own_rows, panel_cols), jnp.float32)], 0)
    head = lax.dynamic_slice_in_dim(padded, jnp.minimum(start, panel_cols), own_rows)
    global_row = start + lax.broadcasted_iota(jnp.int32, (own_rows, 1), 0)
    return jnp.where(global_row < panel_cols, head, rows)


def solution(mesh):
    placed = (
        P(("scen", "grp"), None, None),
        P(("scen", "grp"), None, None),
        P(("scen", "grp")),
        P(),
    )
    whole = mesh.shape["scen"] == 8 and mesh.shape["grp"] == 4
    return jax.shard_map(
        on_slice if whole else any_mesh,
        mesh=mesh,
        in_specs=placed,
        out_specs=P("scen", None),
        check_vma=False,
    )
```

time: 279 us -> 138 us (0.49)
  the two profiles are of different devices: /device:TPU:0 before, /device:TPU:6 now
where the time goes in v2:
time: 138 us; the launch traced here: 137 us
  Pallas kernels  65.3 us (47%)
  waiting for transfers between devices  42.7 us (31%)
  starting transfers between devices  20.6 us (15%)
  local copies, waits for them, and re-layouts  5.87 us (4%)
  other arithmetic  1.75 us (1%)
    ppermute x22, waiting for transfers between devices, flip(): return lax.ppermute(array, axis, [(i, i ^ mask) for i in range(size)])  42.7 us
    pallas_call x1, Pallas kernels, scen_solve(): pl.pallas_call(scen_kernel, out_shape=jax.ShapeDtypeStruct((cols, n), jnp...  28.3 us
    ppermute x22, starting transfers between devices, flip(): return lax.ppermute(array, axis, [(i, i ^ mask) for i in range(size)])  20.6 us
    pallas_call x2, Pallas kernels, panel_products(): pl.pallas_call(products_kernel, out_shape=[jax.ShapeDtypeStruct(shape, jn...  13.2 us
    pallas_call x1, Pallas kernels, pivot_two(): pl.pallas_call(pivot_two_kernel, out_shape=[sd(2 * half, half), sd(half,...  8.77 us
    pallas_call x1, Pallas kernels, pivot_one(): pl.pallas_call(pivot_one_kernel, out_shape=[sd(n // 2, n // 2), sd(n, n /...  8.43 us
    pallas_call x2, Pallas kernels, final_rows(): pl.pallas_call(lambda *refs: final_kernel(*refs, part=part), out_shape=ja...  4.54 us
    unnamed x12, local copies, waits for them, and re-layouts  2.85 us
  transfers between devices with their start and end apart: 22, of which 11 were waited for; matrix products, arithmetic and copies ran while one was open for 2% of the time, Pallas kernels for 19%

profile of v2, /device:TPU:6, one launch (start us, length us, event | category | flops | bytes accessed | tf_op | source)
XLA Modules:
  0.0 137.3 jit_solution(1118250118658034310)
XLA Ops:
  0.7 0.6 stack.86.where_ref
  1.3 0.6 stack.81.where_ref
  1.9 0.1 stack.77.perm_ref
  2.0 1.3 copy-done.2
  3.2 28.3 %scen_solve.1.xt_ref = bf16[512,768]{1,0:T(8,128)(2,1)S(1)} custom-call(s32[1]{0:T(128)S(6)} %copy.7.act_ref, bf16[1,768,768]{2,1,0:T(8,128)(2,1)S(1)} %copy-done.2, bf16[1,768,4096]{2,1,0:T(8,128)(2,1)} %c_ref.5), custom_call_target="tpu_custom_call" | custom-call | tf_op jit(solution)/shard_map/scen_solve/pallas_call | solution.py:131
  31.6 2.1 %pivot_prod.1.packed_ref = f32[320,512]{1,0:T(8,128)S(1)} custom-call(bf16[512,768]{1,0:T(8,128)(2,1)S(1)} %scen_solve.1.xt_ref, bf16[1,768,4096]{2,1,0:T(8,128)(2,1)} %c_ref.5), custom_call_target="tpu_custom_call" | custom-call | flops 402653184 | bytes 2228224 | tf_op jit(solution)/shard_map/pivot_prod/pallas_call | solution.py:165
  33.7 0.8 copy-done.1
  34.5 6.6 %panel_products.2 = (f32[8,96,512]{2,1,0:T(8,128)}, f32[2,2,2,96,512]{4,3,2,1,0:T(8,128)}, f32[2,4,88,512]{3,2,1,0:T(8,128)}) custom-call(s32[5]{0:T(128)} %stack.86.where_ref, bf16[512,768]{1,0:T(8,128)(2,1)} %copy-done, bf16[1,768,4096]{2,1,0:T(8,128)(2,1)} %c_ref.5, f32[320,512]{1,0:T(8,128)} %copy-done.1), custom_call_target="tpu_custom_call" | custom-call | flops 1610612736 | bytes 11534336 | tf_op jit(solution)/shard_map/panel_products/pallas_call | solution.py:278
  41.2 0.5 collective-permute-start.1
  41.7 6.6 %panel_products.3 = (f32[8,96,512]{2,1,0:T(8,128)}, f32[2,2,2,96,512]{4,3,2,1,0:T(8,128)}, f32[2,4,88,512]{3,2,1,0:T(8,128)}) custom-call(s32[5]{0:T(128)} %stack.81.where_ref, bf16[512,768]{1,0:T(8,128)(2,1)} %copy-done, bf16[1,768,4096]{2,1,0:T(8,128)(2,1)} %c_ref.5, f32[320,512]{1,0:T(8,128)} %copy-done.1), custom_call_target="tpu_custom_call" | custom-call | flops 1610612736 | bytes 11534336 | tf_op jit(solution)/shard_map/panel_products/pallas_call | solution.py:278
  48.3 1.6 %fusion.3 = (f32[1,2,2,96,512]{4,3,2,1,0:T(8,128)S(1)}, f32[1,2,2,96,512]{4,3,2,1,0:T(8,128)S(1)}) fusion(f32[2,2,2,96,512]{4,3,2,1,0:T(8,128)} %get-tuple-element.53), kind=kLoop, calls=%fused_computation.32 | loop fusion | bytes 3145728 | tf_op jit(solution)/shard_map/slice | solution.py:365
  49.9 0.2 copy-done.4
  50.1 0.1 slice_add_fusion
  50.3 0.6 collective-permute-start.3
  50.9 0.2 bitcast_add_fusion.1
  51.1 0.5 copy-done.5
  51.6 0.1 bitcast_add_fusion.3
  51.8 1.6 %collective-permute-start.5 = (f32[4,88,512]{2,1,0:T(8,128)S(1)}, f32[4,88,512]{2,1,0:T(8,128)S(1)}, u32[]{:S(2)}, u32[]{:S(2)}) collective-permute-start(f32[4,88,512]{2,1,0:T(8,128)S(1)} %bitcast_add_fusion.3), channel_id=1, source_target_pairs={{0,1},{1,0},{2,3},{3,2},{4,5},{5,4},{6,7},{7,6},{8,9},{9,8},{10,11... | collective-permute-start | bytes 2162696 | tf_op jit(solution)/shard_map/ppermute | solution.py:250
  53.4 0.4 bitcast_add_fusion
  53.8 0.1 bitcast_add_fusion.2
  53.9 16.4 %collective-permute-done.3 = f32[4,96,512]{2,1,0:T(8,128)S(1)} collective-permute-done((f32[4,96,512]{2,1,0:T(8,128)S(1)}, f32[4,96,512]{2,1,0:T(8,128)S(1)}, u32[]{:S(2)}, u32[]{:S(2)}) %collective-permute-start.3) | collective-permute-done | bytes 786464 | tf_op jit(solution)/shard_map/ppermute | solution.py:250
  70.4 0.4 collective-permute-done.4
  70.9 1.6 %collective-permute-start.9 = (f32[2,88,512]{2,1,0:T(8,128)S(1)}, f32[2,88,512]{2,1,0:T(8,128)S(1)}, u32[]{:S(2)}, u32[]{:S(2)}) collective-permute-start(f32[2,88,512]{2,1,0:T(8,128)S(1)} %slice_add_fusion.7), channel_id=1, source_target_pairs={{0,8},{4,12},{8,0},{12,4},{16,24},{20,28},{24,16},{28,20},{1,9},{5... | collective-permute-start | bytes 1081352 | tf_op jit(solution)/shard_map/ppermute | solution.py:250
  72.5 1.6 %collective-permute-start.8 = (f32[2,96,512]{2,1,0:T(8,128)S(1)}, f32[2,96,512]{2,1,0:T(8,128)S(1)}, u32[]{:S(2)}, u32[]{:S(2)}) collective-permute-start(f32[2,96,512]{2,1,0:T(8,128)S(1)} %slice_add_fusion.3), channel_id=1, source_target_pairs={{0,1},{1,0},{2,3},{3,2},{4,5},{5,4},{6,7},{7,6},{8,9},{9,8},{10,11... | collective-permute-start | bytes 1179656 | tf_op jit(solution)/shard_map/ppermute | solution.py:250
  74.1 0.5 collective-permute-start.6
  74.7 9.2 %collective-permute-done.6 = f32[2,96,512]{2,1,0:T(8,128)S(1)} collective-permute-done((f32[2,96,512]{2,1,0:T(8,128)S(1)}, f32[2,96,512]{2,1,0:T(8,128)S(1)}, u32[]{:S(2)}, u32[]{:S(2)}) %collective-permute-start.6) | collective-permute-done | bytes 393248 | tf_op jit(solution)/shard_map/ppermute | solution.py:250
  84.0 0.5 collective-permute-start.7
  84.5 1.6 %collective-permute-start.11 = (f32[1,72,512]{2,1,0:T(8,128)S(1)}, f32[1,72,512]{2,1,0:T(8,128)S(1)}, u32[]{:S(2)}, u32[]{:S(2)}) collective-permute-start(f32[1,72,512]{2,1,0:T(8,128)S(1)} %slice_add_fusion.12), channel_id=1, source_target_pairs={{0,1},{1,0},{2,3},{3,2},{4,5},{5,4},{6,7},{7,6},{8,9},{9,8},{10,11... | collective-permute-start | bytes 442376 | tf_op jit(solution)/shard_map/ppermute | solution.py:250
  86.2 0.6 collective-permute-start.13
  86.8 0.6 collective-permute-start.12
  87.5 1.0 collective-permute-done.7
  88.5 2.9 %collective-permute-start.10 = (f32[40,512]{1,0:T(8,128)S(1)}, f32[40,512]{1,0:T(8,128)S(1)}, u32[]{:S(2)}, u32[]{:S(2)}) collective-permute-start(f32[40,512]{1,0:T(8,128)S(1)} %fusion.2), channel_id=1, source_target_pairs={{0,2},{1,3},{2,0},{3,1},{4,6},{5,7},{6,4},{7,5},{8,10},{9,11},{10,... | collective-permute-start | bytes 245768 | tf_op jit(solution)/shard_map/ppermute | solution.py:250
  91.5 0.3 collective-permute-done.13
  91.8 0.7 collective-permute-done.12
  92.7 2.0 %collective-permute-done.10 = f32[40,512]{1,0:T(8,128)S(1)} collective-permute-done((f32[40,512]{1,0:T(8,128)S(1)}, f32[40,512]{1,0:T(8,128)S(1)}, u32[]{:S(2)}, u32[]{:S(2)}) %collective-permute-start.10) | collective-permute-done | bytes 81952 | tf_op jit(solution)/shard_map/ppermute | solution.py:250
  94.7 1.5 %collective-permute-start.16 = (f32[40,512]{1,0:T(8,128)S(1)}, f32[40,512]{1,0:T(8,128)S(1)}, u32[]{:S(2)}, u32[]{:S(2)}) collective-permute-start(f32[40,512]{1,0:T(8,128)S(1)} %add.167), channel_id=1, source_target_pairs={{0,24},{4,28},{8,16},{12,20},{16,8},{20,12},{24,0},{28,4},{1,25},{... | collective-permute-start | bytes 245768 | tf_op jit(solution)/shard_map/ppermute | solution.py:250
  96.2 0.5 collective-permute-start.15
  96.8 1.5 %collective-permute-start.14 = (f32[40,512]{1,0:T(8,128)S(1)}, f32[40,512]{1,0:T(8,128)S(1)}, u32[]{:S(2)}, u32[]{:S(2)}) collective-permute-start(f32[40,512]{1,0:T(8,128)S(1)} %add.167), channel_id=1, source_target_pairs={{0,8},{4,12},{8,0},{12,4},{16,24},{20,28},{24,16},{28,20},{1,9},{5... | collective-permute-start | bytes 245768 | tf_op jit(solution)/shard_map/ppermute | solution.py:250
  98.3 2.1 %collective-permute-start.17 = (f32[256,256]{1,0:T(8,128)S(1)}, f32[256,256]{1,0:T(8,128)S(1)}, u32[]{:S(2)}, u32[]{:S(2)}) collective-permute-start(f32[256,256]{1,0:T(8,128)S(1)} %get-tuple-element.92), channel_id=1, source_target_pairs={{0,2},{1,3},{2,0},{3,1},{4,6},{5,7},{6,4},{7,5},{8,10},{9,11},{10,... | collective-permute-start | bytes 786440 | tf_op jit(solution)/shard_map/ppermute | solution.py:250
  100.4 0.6 collective-permute-done.15
  101.0 0.2 collective-permute-done.14
  101.4 10.9 %collective-permute-done.17 = f32[256,256]{1,0:T(8,128)S(1)} collective-permute-done((f32[256,256]{1,0:T(8,128)S(1)}, f32[256,256]{1,0:T(8,128)S(1)}, u32[]{:S(2)}, u32[]{:S(2)}) %collective-permute-start.17) | collective-permute-done | bytes 262176 | tf_op jit(solution)/shard_map/ppermute | solution.py:250
  112.5 8.4 %pivot_one.1 = (f32[256,256]{1,0:T(8,128)S(1)}, f32[512,256]{1,0:T(8,128)S(1)}, f32[256,256]{1,0:T(8,128)S(1)}, f32[256,256]{1,0:T(8,128)S(1)}) custom-call(s32[8]{0:T(128)S(1)} %stack.77.perm_ref, f32[1,512]{1,0:T(1,128)S(1)} %bitcast.38, f32[160,512]{1,0:T(8,128)S(1)} %pad_maximum_fusion.1.refs_0_, f32[160,512]{1,0:T(8,128)S(1)} %collective-permute-done.18.refs_1_), custom_call_target="tpu_custom_call" | custom-call | flops 10000000000 | bytes 4194304 | tf_op jit(solution)/shard_map/pivot_one/pallas_call | solution.py:219
  121.0 1.0 collective-permute-done.19
  122.0 1.9 %collective-permute-start.20 = (f32[256,256]{1,0:T(8,128)S(1)}, f32[256,256]{1,0:T(8,128)S(1)}, u32[]{:S(2)}, u32[]{:S(2)}) collective-permute-start(f32[256,256]{1,0:T(8,128)S(1)} %slice_add_fusion.16.refs_5_), channel_id=1, source_target_pairs={{0,1},{1,0},{2,3},{3,2},{4,5},{5,4},{6,7},{7,6},{8,9},{9,8},{10,11... | collective-permute-start | bytes 786440 | tf_op jit(solution)/shard_map/ppermute | solution.py:250
  123.9 8.8 %pivot_two.1 = (f32[512,256]{1,0:T(8,128)S(1)}, f32[256,256]{1,0:T(8,128)S(1)}) custom-call(f32[256,256]{1,0:T(8,128)S(1)} %get-tuple-element.79.wt1_ref.refs_1_, f32[256,256]{1,0:T(8,128)S(1)} %get-tuple-element.80.u_ref, f32[256,256]{1,0:T(8,128)S(1)} %get-tuple-element.81.rest_ref), custom_call_target="tpu_custom_call" | custom-call | flops 10000000000 | bytes 4194304 | tf_op jit(solution)/shard_map/pivot_two/pallas_call | solution.py:233
  132.7 2.3 %owned_rows.2.refs_7_ = f32[512,512]{1,0:T(8,128)} custom-call(s32[2]{0:T(128)S(1)} %pad_add_fusion.refs_0_, f32[256,256]{1,0:T(8,128)S(1)} %get-tuple-element.79.wt1_ref.refs_1_, f32[512,256]{1,0:T(8,128)S(1)} %get-tuple-element.82.refs_2_, f32[512,256]{1,0:T(8,128)S(1)} %get-tuple-element.83.refs_3_, f32[256,256]{1,0:T(8,128)S(1)} %get-tuple-element.84.refs_4_, ...), custom_call_target="tpu_custom_call" | custom-call | tf_op jit(solution)/shard_map/owned_rows/pallas_call | solution.py:325
  135.0 2.3 %owned_rows.3 = f32[512,512]{1,0:T(8,128)} custom-call(s32[2]{0:T(128)S(1)} %pad_add_fusion.refs_0_, f32[256,256]{1,0:T(8,128)S(1)} %get-tuple-element.79.wt1_ref.refs_1_, f32[512,256]{1,0:T(8,128)S(1)} %get-tuple-element.82.refs_2_, f32[512,256]{1,0:T(8,128)S(1)} %get-tuple-element.83.refs_3_, ...), custom_call_target="tpu_custom_call", output_to_operand_aliasing={{}: (7, {})} | custom-call | tf_op jit(solution)/shard_map/owned_rows/pallas_call | solution.py:325
  (52 shorter events, 1.2 us)
Async XLA Ops:
  2.0 1.3 copy-start.2
  31.6 2.1 %copy-start = (bf16[512,768]{1,0:T(8,128)(2,1)}, bf16[512,768]{1,0:T(8,128)(2,1)S(1)}, u32[]{:S(2)}) copy-start(bf16[512,768]{1,0:T(8,128)(2,1)S(1)} %scen_solve.1.xt_ref) | copy-start | bytes 2359300
  33.7 0.9 copy-start.1
  41.2 8.8 %collective-permute-start = (f32[8,96,512]{2,1,0:T(8,128)}, f32[8,96,512]{2,1,0:T(8,128)S(1)}, u32[]{:S(2)}, u32[]{:S(2)}) collective-permute-start(f32[8,96,512]{2,1,0:T(8,128)} %get-tuple-element.48), channel_id=1, source_target_pairs={{0,4},{4,0},{8,12},{12,8},{16,20},{20,16},{24,28},{28,24},{1,5},{5... | collective-permute-start | bytes 4718600 | tf_op jit(solution)/shard_map/ppermute | solution.py:250
  41.2 9.7 %collective-permute-start.1 = (f32[8,96,512]{2,1,0:T(8,128)}, f32[8,96,512]{2,1,0:T(8,128)S(1)}, u32[]{:S(2)}, u32[]{:S(2)}) collective-permute-start(f32[8,96,512]{2,1,0:T(8,128)} %bitcast.39), channel_id=1, source_target_pairs={{0,4},{4,0},{8,12},{12,8},{16,20},{20,16},{24,28},{28,24},{1,5},{5... | collective-permute-start | bytes 4718600 | tf_op jit(solution)/shard_map/ppermute | solution.py:250
  41.7 9.5 %collective-permute-start.2 = (f32[8,88,512]{2,1,0:T(8,128)}, f32[8,88,512]{2,1,0:T(8,128)S(1)}, u32[]{:S(2)}, u32[]{:S(2)}) collective-permute-start(f32[8,88,512]{2,1,0:T(8,128)} %bitcast.40), channel_id=1, source_target_pairs={{0,4},{4,0},{8,12},{12,8},{16,20},{20,16},{24,28},{28,24},{1,5},{5... | collective-permute-start | bytes 4325384 | tf_op jit(solution)/shard_map/ppermute | solution.py:250
  48.3 1.9 %copy-start.4 = (f32[8,96,512]{2,1,0:T(8,128)S(1)}, f32[8,96,512]{2,1,0:T(8,128)}, u32[]{:S(2)}) copy-start(f32[8,96,512]{2,1,0:T(8,128)} %get-tuple-element.52) | copy-start | bytes 4718596
  50.3 1.4 copy-start.5
  50.3 20.0 %collective-permute-start.3 = (f32[4,96,512]{2,1,0:T(8,128)S(1)}, f32[4,96,512]{2,1,0:T(8,128)S(1)}, u32[]{:S(2)}, u32[]{:S(2)}) collective-permute-start(f32[4,96,512]{2,1,0:T(8,128)S(1)} %slice_add_fusion), channel_id=1, source_target_pairs={{0,8},{4,12},{8,0},{12,4},{16,24},{20,28},{24,16},{28,20},{1,9},{5... | collective-permute-start | bytes 2359304 | tf_op jit(solution)/shard_map/ppermute | solution.py:250
  51.1 19.7 %collective-permute-start.4 = (f32[4,96,512]{2,1,0:T(8,128)S(1)}, f32[4,96,512]{2,1,0:T(8,128)S(1)}, u32[]{:S(2)}, u32[]{:S(2)}) collective-permute-start(f32[4,96,512]{2,1,0:T(8,128)S(1)} %bitcast_add_fusion.1), channel_id=1, source_target_pairs={{0,16},{4,20},{8,24},{12,28},{16,0},{20,4},{24,8},{28,12},{1,17},{... | collective-permute-start | bytes 2359304 | tf_op jit(solution)/shard_map/ppermute | solution.py:250
  51.8 19.1 %collective-permute-start.5 = (f32[4,88,512]{2,1,0:T(8,128)S(1)}, f32[4,88,512]{2,1,0:T(8,128)S(1)}, u32[]{:S(2)}, u32[]{:S(2)}) collective-permute-start(f32[4,88,512]{2,1,0:T(8,128)S(1)} %bitcast_add_fusion.3), channel_id=1, source_target_pairs={{0,1},{1,0},{2,3},{3,2},{4,5},{5,4},{6,7},{7,6},{8,9},{9,8},{10,11... | collective-permute-start | bytes 2162696 | tf_op jit(solution)/shard_map/ppermute | solution.py:250
  70.9 15.3 %collective-permute-start.9 = (f32[2,88,512]{2,1,0:T(8,128)S(1)}, f32[2,88,512]{2,1,0:T(8,128)S(1)}, u32[]{:S(2)}, u32[]{:S(2)}) collective-permute-start(f32[2,88,512]{2,1,0:T(8,128)S(1)} %slice_add_fusion.7), channel_id=1, source_target_pairs={{0,8},{4,12},{8,0},{12,4},{16,24},{20,28},{24,16},{28,20},{1,9},{5... | collective-permute-start | bytes 1081352 | tf_op jit(solution)/shard_map/ppermute | solution.py:250
  72.5 13.7 %collective-permute-start.8 = (f32[2,96,512]{2,1,0:T(8,128)S(1)}, f32[2,96,512]{2,1,0:T(8,128)S(1)}, u32[]{:S(2)}, u32[]{:S(2)}) collective-permute-start(f32[2,96,512]{2,1,0:T(8,128)S(1)} %slice_add_fusion.3), channel_id=1, source_target_pairs={{0,1},{1,0},{2,3},{3,2},{4,5},{5,4},{6,7},{7,6},{8,9},{9,8},{10,11... | collective-permute-start | bytes 1179656 | tf_op jit(solution)/shard_map/ppermute | solution.py:250
  74.1 9.9 %collective-permute-start.6 = (f32[2,96,512]{2,1,0:T(8,128)S(1)}, f32[2,96,512]{2,1,0:T(8,128)S(1)}, u32[]{:S(2)}, u32[]{:S(2)}) collective-permute-start(f32[2,96,512]{2,1,0:T(8,128)S(1)} %slice_add_fusion.4), channel_id=1, source_target_pairs={{0,16},{4,20},{8,24},{12,28},{16,0},{20,4},{24,8},{28,12},{1,17},{... | collective-permute-start | bytes 1179656 | tf_op jit(solution)/shard_map/ppermute | solution.py:250
  84.0 4.5 %collective-permute-start.7 = (f32[40,512]{1,0:T(8,128)S(1)}, f32[40,512]{1,0:T(8,128)S(1)}, u32[]{:S(2)}, u32[]{:S(2)}) collective-permute-start(f32[40,512]{1,0:T(8,128)S(1)} %pad_maximum_fusion.2), channel_id=1, source_target_pairs={{0,1},{1,0},{2,3},{3,2},{4,5},{5,4},{6,7},{7,6},{8,9},{9,8},{10,11... | collective-permute-start | bytes 245768 | tf_op jit(solution)/shard_map/ppermute | solution.py:250
  84.5 6.9 %collective-permute-start.11 = (f32[1,72,512]{2,1,0:T(8,128)S(1)}, f32[1,72,512]{2,1,0:T(8,128)S(1)}, u32[]{:S(2)}, u32[]{:S(2)}) collective-permute-start(f32[1,72,512]{2,1,0:T(8,128)S(1)} %slice_add_fusion.12), channel_id=1, source_target_pairs={{0,1},{1,0},{2,3},{3,2},{4,5},{5,4},{6,7},{7,6},{8,9},{9,8},{10,11... | collective-permute-start | bytes 442376 | tf_op jit(solution)/shard_map/ppermute | solution.py:250
  86.2 5.6 %collective-permute-start.13 = (f32[1,88,512]{2,1,0:T(8,128)S(1)}, f32[1,88,512]{2,1,0:T(8,128)S(1)}, u32[]{:S(2)}, u32[]{:S(2)}) collective-permute-start(f32[1,88,512]{2,1,0:T(8,128)S(1)} %slice_add_fusion.11), channel_id=1, source_target_pairs={{0,16},{4,20},{8,24},{12,28},{16,0},{20,4},{24,8},{28,12},{1,17},{... | collective-permute-start | bytes 540680 | tf_op jit(solution)/shard_map/ppermute | solution.py:250
  86.8 5.7 %collective-permute-start.12 = (f32[1,96,512]{2,1,0:T(8,128)S(1)}, f32[1,96,512]{2,1,0:T(8,128)S(1)}, u32[]{:S(2)}, u32[]{:S(2)}) collective-permute-start(f32[1,96,512]{2,1,0:T(8,128)S(1)} %slice_add_fusion.9), channel_id=1, source_target_pairs={{0,8},{4,12},{8,0},{12,4},{16,24},{20,28},{24,16},{28,20},{1,9},{5... | collective-permute-start | bytes 589832 | tf_op jit(solution)/shard_map/ppermute | solution.py:250
  88.5 6.2 %collective-permute-start.10 = (f32[40,512]{1,0:T(8,128)S(1)}, f32[40,512]{1,0:T(8,128)S(1)}, u32[]{:S(2)}, u32[]{:S(2)}) collective-permute-start(f32[40,512]{1,0:T(8,128)S(1)} %fusion.2), channel_id=1, source_target_pairs={{0,2},{1,3},{2,0},{3,1},{4,6},{5,7},{6,4},{7,5},{8,10},{9,11},{10,... | collective-permute-start | bytes 245768 | tf_op jit(solution)/shard_map/ppermute | solution.py:250
  92.6 19.9 %copy-start.3 = (f32[512]{0:T(512)S(1)}, f32[512]{0:T(512)}, u32[]{:S(2)}) copy-start(f32[512]{0:T(512)} %param.7) | copy-start | bytes 6148
  94.7 5.7 %collective-permute-start.16 = (f32[40,512]{1,0:T(8,128)S(1)}, f32[40,512]{1,0:T(8,128)S(1)}, u32[]{:S(2)}, u32[]{:S(2)}) collective-permute-start(f32[40,512]{1,0:T(8,128)S(1)} %add.167), channel_id=1, source_target_pairs={{0,24},{4,28},{8,16},{12,20},{16,8},{20,12},{24,0},{28,4},{1,25},{... | collective-permute-start | bytes 245768 | tf_op jit(solution)/shard_map/ppermute | solution.py:250
  96.2 4.7 %collective-permute-start.15 = (f32[40,512]{1,0:T(8,128)S(1)}, f32[40,512]{1,0:T(8,128)S(1)}, u32[]{:S(2)}, u32[]{:S(2)}) collective-permute-start(f32[40,512]{1,0:T(8,128)S(1)} %add.167), channel_id=1, source_target_pairs={{0,16},{4,20},{8,24},{12,28},{16,0},{20,4},{24,8},{28,12},{1,17},{... | collective-permute-start | bytes 245768 | tf_op jit(solution)/shard_map/ppermute | solution.py:250
  96.8 4.4 %collective-permute-start.14 = (f32[40,512]{1,0:T(8,128)S(1)}, f32[40,512]{1,0:T(8,128)S(1)}, u32[]{:S(2)}, u32[]{:S(2)}) collective-permute-start(f32[40,512]{1,0:T(8,128)S(1)} %add.167), channel_id=1, source_target_pairs={{0,8},{4,12},{8,0},{12,4},{16,24},{20,28},{24,16},{28,20},{1,9},{5... | collective-permute-start | bytes 245768 | tf_op jit(solution)/shard_map/ppermute | solution.py:250
  98.3 14.0 %collective-permute-start.17 = (f32[256,256]{1,0:T(8,128)S(1)}, f32[256,256]{1,0:T(8,128)S(1)}, u32[]{:S(2)}, u32[]{:S(2)}) collective-permute-start(f32[256,256]{1,0:T(8,128)S(1)} %get-tuple-element.92), channel_id=1, source_target_pairs={{0,2},{1,3},{2,0},{3,1},{4,6},{5,7},{6,4},{7,5},{8,10},{9,11},{10,... | collective-permute-start | bytes 786440 | tf_op jit(solution)/shard_map/ppermute | solution.py:250
  101.2 11.3 %collective-permute-start.18 = (f32[160,512]{1,0:T(8,128)S(1)}, f32[160,512]{1,0:T(8,128)S(1)}, u32[]{:S(2)}, u32[]{:S(2)}) collective-permute-start(f32[160,512]{1,0:T(8,128)S(1)} %pad_maximum_fusion.1.refs_0_), channel_id=1, source_target_pairs={{0,4},{4,0},{8,12},{12,8},{16,20},{20,16},{24,28},{28,24},{1,5},{5... | collective-permute-start | bytes 983048 | tf_op jit(solution)/shard_map/ppermute | solution.py:250
  112.3 20.3 %collective-permute-start.21 = (f32[256,256]{1,0:T(8,128)S(1)}, f32[256,256]{1,0:T(8,128)S(1)}, u32[]{:S(2)}, u32[]{:S(2)}) collective-permute-start(f32[256,256]{1,0:T(8,128)S(1)} %slice_add_fusion.17.refs_5_), channel_id=1, source_target_pairs={{0,1},{1,0},{2,3},{3,2},{4,5},{5,4},{6,7},{7,6},{8,9},{9,8},{10,11... | collective-permute-start | bytes 786440 | tf_op jit(solution)/shard_map/ppermute | solution.py:250
  112.4 9.5 %collective-permute-start.19 = (f32[256,256]{1,0:T(8,128)S(1)}, f32[256,256]{1,0:T(8,128)S(1)}, u32[]{:S(2)}, u32[]{:S(2)}) collective-permute-start(f32[256,256]{1,0:T(8,128)S(1)} %get-tuple-element.85), channel_id=1, source_target_pairs={{0,2},{1,3},{2,0},{3,1},{4,6},{5,7},{6,4},{7,5},{8,10},{9,11},{10,... | collective-permute-start | bytes 786440 | tf_op jit(solution)/shard_map/ppermute | solution.py:250
  122.0 13.0 %collective-permute-start.20 = (f32[256,256]{1,0:T(8,128)S(1)}, f32[256,256]{1,0:T(8,128)S(1)}, u32[]{:S(2)}, u32[]{:S(2)}) collective-permute-start(f32[256,256]{1,0:T(8,128)S(1)} %slice_add_fusion.16.refs_5_), channel_id=1, source_target_pairs={{0,1},{1,0},{2,3},{3,2},{4,5},{5,4},{6,7},{7,6},{8,9},{9,8},{10,11... | collective-permute-start | bytes 786440 | tf_op jit(solution)/shard_map/ppermute | solution.py:250

commit v3 on v2

v3 whole, which is shorter than its diff:
```python
import functools

import jax
import jax.numpy as jnp
from jax import lax
from jax.experimental import pallas as pl
from jax.experimental.pallas import tpu as pltpu
from jax.sharding import PartitionSpec as P

PW = 256
HALF = 256
CUTS = (0, 72, 168, 256)
UNIT = 40
FIRST = 24
H=lax.Precision.HIGHEST
def bc(x,s): return jnp.broadcast_to(x[s:s+1,:], x.shape)
def halves(x):
    hi=x.astype(jnp.bfloat16)
    return hi,(x-hi.astype(jnp.float32)).astype(jnp.bfloat16)
def dot3(a,b,dims):
    (i,),(j,)=dims
    ah,al=halves(a); bh,bl=halves(b)
    return lax.dot_general(jnp.concatenate([ah,ah,al],i),jnp.concatenate([bh,bl,bh],j),(dims,((),())),preferred_element_type=jnp.float32)
def elim(R, off, nb):
    ng=nb//8; nh=len(R[0])
    row=lax.broadcasted_iota(jnp.int32,(8,128),0)
    L={}
    for j in range(nb):
        for g in range(j//8,ng):
            L[j,g]=jnp.broadcast_to(R[g][0][:,off+j:off+j+1],(8,128))
    out=[None]*ng
    a=bc(L[0,0],0); b=bc(L[0,0],1); c=bc(L[1,0],1)
    for j in range(0,nb,2):
        gj=j//8; s=j%8
        det=a*c-b*b
        rd=1.0/det
        al={}; be={}
        for g in range(gj,ng):
            x=L[j,g]*c-L[j+1,g]*b; y=L[j+1,g]*a-L[j,g]*b
            if g==gj:
                x=jnp.where(row>s+1,x,0.0); y=jnp.where(row>s+1,y,0.0)
            al[g]=x; be[g]=y
        nxt=None
        if j+2<nb:
            k=j+2; g=k//8; t=k%8
            p,q,p2,q2=bc(L[j,g],t),bc(L[j+1,g],t),bc(L[j,g],t+1),bc(L[j+1,g],t+1)
            x,y,x2,y2=bc(al[g],t),bc(be[g],t),bc(al[g],t+1),bc(be[g],t+1)
            nxt=(bc(L[k,g],t)-(x*p+y*q)*rd, bc(L[k,g],t+1)-(x2*p+y2*q)*rd, bc(L[k+1,g],t+1)-(x2*p2+y2*q2)*rd)
        for k in range(j+2,nb):
            p=bc(L[j,k//8],k%8); q=bc(L[j+1,k//8],k%8)
            for g in range(k//8,ng):
                L[k,g]=L[k,g]-(al[g]*p+be[g]*q)*rd
        r1=[bc(R[gj][h],s) for h in range(nh)]; r2=[bc(R[gj][h],s+1) for h in range(nh)]
        ra=1.0/a
        sa=lax.rsqrt(a); sb=lax.rsqrt(det*ra); ba=b*ra
        if s==0: out[gj]=[jnp.zeros((8,128),jnp.float32)]*nh
        for h in range(nh):
            out[gj][h]=jnp.where(row==s,r1[h]*sa,jnp.where(row==s+1,(r2[h]-ba*r1[h])*sb,out[gj][h]))
        for g in range(gj,ng):
            if g==gj and s==6: continue
            x=al[g]*rd; y=be[g]*rd
            R[g]=[R[g][h]-(x*r1[h]+y*r2[h]) for h in range(nh)]
        if nxt: a,b,c=nxt
    return out
def base128(A, exact=False, nb=32, between=None):
    row=lax.broadcasted_iota(jnp.int32,(8,128),0); lane=lax.broadcasted_iota(jnp.int32,(8,128),1)
    M=[[A[8*g:8*g+8,:],jnp.where(lane==row+8*g,1.0,0.0)] for g in range(16)]
    outs=[]
    n=128//nb; ng=nb//8
    for c in range(n):
        if between: between[c]()
        o=elim(M[c*ng:(c+1)*ng],c*nb,nb)
        outs+=o
        if c<n-1:
            O=[jnp.concatenate([o[g][h] for g in range(ng)],0) for h in range(2)]
            O2=jnp.concatenate(O,1)
            dims=((0,),(0,))
            if exact: T=lax.dot_general(O[0],O2,(dims,((),())),precision=H,preferred_element_type=jnp.float32)
            else: T=dot3(O[0],O2,dims)
            for g in range((c+1)*ng,16):
                M[g]=[M[g][h]-T[8*g:8*g+8,128*h:128*h+128] for h in range(2)]
    return [jnp.concatenate([outs[g][h] for g in range(16)],0) for h in range(2)]
BS=128
def dotT(a,b,prec=H): return lax.dot_general(a,b,(((0,),(0,)),((),())),precision=prec,preferred_element_type=jnp.float32)
def dot(a,b,prec=H): return lax.dot_general(a,b,(((1,),(0,)),((),())),precision=prec,preferred_element_type=jnp.float32)
def blk(k): return slice(k*BS,(k+1)*BS)
def sym(a): return 0.5*(a+a.T)
def upper_blocks(m): return [(i,j) for i in range(m) for j in range(i,m)]
def packed_places(m):
    places,slots={},[]
    blocks=upper_blocks(m)
    full=len(blocks)//m*m
    for q,ij in enumerate(blocks[:full]): places[ij]=[(0,q//m*BS,q%m,BS)]
    rest=blocks[full:]
    cut=BS*len(rest)//m
    for q,ij in enumerate(rest):
        per=BS//cut
        places[ij]=[(t*cut,full//m*BS,q*per+t,cut) for t in range(per)]
    return places,full//m*BS+(cut if rest else 0)
def lanes(g): return slice(g*BS,(g+1)*BS)
def fetch_slabs(ids_ref,core_bit,c_hbm,slabs,sems):
    own=slabs.shape[2]
    copies=[]
    for s in range(4):
        slab=ids_ref[0]^(s%2*4+s//2*2+core_bit)
        cols=pl.ds(pl.multiple_of(slab*own,own),own)
        copies.append(pltpu.make_async_copy(c_hbm.at[0,:,cols],slabs.at[s],sems.at[s]))
        copies[-1].start()
    return copies
def slab_products(ids_ref,core_bit,xt_ref,packed_ref,slabs,copies,stages,outs,sems):
    a,b,z=stages
    main,rest=CUTS[1],UNIT-FIRST
    pending=[]
    for s in range(4):
        slab=ids_ref[0]^(s%2*4+s//2*2+core_bit)
        copies[s].wait()
        total=dot(xt_ref[...],slabs[s],None)
        for half in range(2):
            to=pl.ds(ids_ref[1]^half,1)
            part=total[half*HALF:(half+1)*HALF,:]
            a[s,to,:main,:]=part[CUTS[0]:CUTS[1],:][None]
            b[s,to]=part[CUTS[1]:CUTS[2],:][None]
            z[s,to]=part[CUTS[2]:CUTS[3],:][None]
        unit=pl.multiple_of(slab*UNIT,8)
        a[s,0,main:,:]=packed_ref[pl.ds(unit,FIRST),:]
        a[s,1,main:main+rest,:]=packed_ref[pl.ds(unit+FIRST,rest),:]
        a[s,1,main+rest:,:]=jnp.zeros((FIRST-rest,a.shape[3]),jnp.float32)
        x,y=s//2,s%2
        to=(outs[0].at[x,y],outs[1].at[y,:,x],outs[2].at[:,x,y])
        for i in range(3):
            pending.append(pltpu.make_async_copy(stages[i].at[s],to[i],sems.at[s,i]))
            pending[-1].start()
    for copy in pending: copy.wait()
def slab_shapes(own):
    high=[CUTS[1]+FIRST,CUTS[2]-CUTS[1],CUTS[3]-CUTS[2]]
    outs=[jax.ShapeDtypeStruct((2,2,2,h,own),jnp.float32) for h in high]
    stages=[pltpu.VMEM((4,2,h,own),jnp.float32) for h in high]
    return outs,stages
def pack_pivot(x,panel,packed_ref):
    n=x.shape[0]; half=n//2; per=half//BS
    T=dot(x,panel,None)
    D=[sym(T[:half,:half]),sym(T[half:,half:])]
    for (i,j),where in packed_places(n//BS)[0].items():
        if i//per==j//per: v=D[i//per][blk(i%per),blk(j%per)]
        else: v=T[blk(i),blk(j)]
        for r,row,g,rows in where: packed_ref[row:row+rows,lanes(g)]=v[r:r+rows,:]
def scen_kernel(ids_ref,act_ref,k_ref,c_hbm,x_ref,packed_ref,*refs,away):
    outs,refs=refs[:3*away],refs[3*away:]
    M,D,Wk,left,right,row_ref,inv_ref,panel_ref,sem=refs[:9]
    n=k_ref.shape[1]; nblk=n//BS
    fetch=pltpu.make_async_copy(c_hbm.at[0,:,0:panel_ref.shape[1]],panel_ref,sem)
    fetch.start()
    if away:
        slabs,stages,in_sems,out_sems=refs[9],refs[10:13],refs[13],refs[14]
        copies=fetch_slabs(ids_ref,1,c_hbm,slabs,in_sems)
    M[...]=k_ref[0].astype(jnp.float32)
    D[...]=k_ref[0,0:BS,0:BS].astype(jnp.float32)
    Wk[...]=jnp.zeros_like(Wk)
    eye=jnp.where(lax.broadcasted_iota(jnp.int32,(BS,BS),0)==lax.broadcasted_iota(jnp.int32,(BS,BS),1),1.0,0.0)
    def sweep(k,live):
        here=pl.ds(pl.multiple_of(k*BS,BS),BS)
        def invert():
            W=Wk[...]
            inv_ref[...]=dotT(W,W)
            col_hi,col_lo=halves(jnp.where(live,M[:,here],0.0))
            left[:,0:BS]=col_hi; left[:,BS:2*BS]=col_hi; left[:,2*BS:]=col_lo
            left[here,:]=jnp.zeros((BS,3*BS),jnp.bfloat16)
        def scale():
            inv=inv_ref[...]
            row=dot3(inv,M[here,:],((1,),(0,)))
            row_ref[...]=row
            row_ref[:,here]=eye-inv
            hi,lo=halves(row_ref[...])
            right[0:BS,:]=hi; right[BS:2*BS,:]=lo; right[2*BS:,:]=hi
            row_ref[...]=row
            row_ref[:,here]=-inv
        def spread(rows):
            M[rows,:]=M[rows,:]-dot(left[rows,:],right[...],None)
        def first(): spread(slice(0,n//2))
        def second():
            spread(slice(n//2,n))
            M[here,:]=jnp.where(live,row_ref[...],M[here,:])
        return invert,scale,first,second
    def step(k,_):
        here=pl.ds(pl.multiple_of(k*BS,BS),BS)
        follow=pl.ds(pl.multiple_of(jnp.minimum(k+1,nblk-1)*BS,BS),BS)
        _,W=base128(D[...],between=sweep(jnp.maximum(k-1,0),k>0))
        P=dot3(W,M[here,follow],((1,),(0,)))
        D[...]=M[follow,follow]-dot3(P,P,((0,),(0,)))
        Wk[...]=W
        return 0
    lax.fori_loop(0,nblk,step,0)
    for part in sweep(nblk-1,True): part()
    fetch.wait()
    panel=panel_ref[...]
    kept=lax.broadcasted_iota(jnp.int32,(n,1),0)<act_ref[0]
    masked=jnp.where(kept,panel,jnp.zeros((),jnp.bfloat16))
    hi,lo=halves(M[...])
    x=dotT(masked,hi,None)+dotT(masked,lo,None)
    kept=lax.broadcasted_iota(jnp.int32,(1,n),1)<act_ref[0]
    x=jnp.where(kept,-x,0.0).astype(jnp.bfloat16)
    x_ref[...]=x
    pack_pivot(x,panel,packed_ref)
    if away: slab_products(ids_ref,1,x_ref,packed_ref,slabs,copies,stages,outs,out_sems)
def scen_solve(ids,kkt,coupling,active,cols,own=0):
    n=kkt.shape[1]
    vm=pltpu.VMEM; dma=pltpu.SemaphoreType.DMA
    smem,vmem,any_=(pl.BlockSpec(memory_space=m) for m in (pltpu.SMEM,vm,pl.ANY))
    out_shape=[jax.ShapeDtypeStruct((cols,n),jnp.bfloat16),jax.ShapeDtypeStruct((packed_places(cols//BS)[1],cols),jnp.float32)]
    scratch=[vm((n,n),jnp.float32),vm((BS,BS),jnp.float32),vm((BS,BS),jnp.float32),vm((n,3*BS),jnp.bfloat16),
        vm((3*BS,n),jnp.bfloat16),vm((BS,n),jnp.float32),vm((BS,BS),jnp.float32),vm((n,cols),jnp.bfloat16),dma]
    if own:
        outs,stages=slab_shapes(own)
        out_shape+=outs
        scratch+=[vm((4,n,own),jnp.bfloat16)]+stages+[dma((4,)),dma((4,3))]
    return pl.pallas_call(functools.partial(scen_kernel,away=bool(own)),
        out_shape=out_shape,in_specs=[smem,smem,vmem,any_],out_specs=[vmem,vmem]+[any_]*(len(out_shape)-2),
        scratch_shapes=scratch,
        compiler_params=pltpu.CompilerParams(vmem_limit_bytes=52*2**20),
        name="scen_solve")(ids,active,kkt,coupling)
def kept_kernel(ids_ref,xt_ref,packed_ref,c_hbm,*refs):
    outs,slabs,stages,in_sems,out_sems=refs[:3],refs[3],refs[4:7],refs[7],refs[8]
    copies=fetch_slabs(ids_ref,0,c_hbm,slabs,in_sems)
    slab_products(ids_ref,0,xt_ref,packed_ref,slabs,copies,stages,outs,out_sems)
def kept_products(ids,xt,packed,coupling,own):
    cols,n=xt.shape
    dma=pltpu.SemaphoreType.DMA
    smem,vmem,any_=(pl.BlockSpec(memory_space=m) for m in (pltpu.SMEM,pltpu.VMEM,pl.ANY))
    outs,stages=slab_shapes(own)
    return pl.pallas_call(kept_kernel,out_shape=outs,in_specs=[smem,vmem,vmem,any_],out_specs=[any_]*3,
        scratch_shapes=[pltpu.VMEM((4,n,own),jnp.bfloat16)]+stages+[dma((4,)),dma((4,3))],
        cost_estimate=pl.CostEstimate(flops=8*own*cols*n,bytes_accessed=8*own*(n+4*cols),transcendentals=0),
        compiler_params=pltpu.CompilerParams(vmem_limit_bytes=40*2**20),
        name="kept_products")(ids,xt,packed,coupling)
def panel_factor(A,wt_ref,l_ref,base):
    n=A.shape[1]; end=base+2*BS
    eye=lax.broadcasted_iota(jnp.int32,(BS,BS),0)<=lax.broadcasted_iota(jnp.int32,(BS,BS),1)
    WT=[]
    for k in range(2):
        lo=base+k*BS; me=slice(lo,lo+BS)
        Uk,Wk=base128(A[me,me])
        WT.append(Wk.T)
        l_ref[lo-base:lo-base+BS,blk(k)]=jnp.where(eye,Uk,0.0).T
        if lo+BS<n:
            P=dot3(Wk,A[me,lo+BS:],((1,),(0,)))
            A[me,lo+BS:]=P
            for i in range((n-lo)//BS-1):
                r=lo+(i+1)*BS
                if r<end: A[r:r+BS,r:]=A[r:r+BS,r:]-dot3(P[:,i*BS:(i+1)*BS],P[:,i*BS:],((0,),(0,)))
                l_ref[r-base:r-base+BS,blk(k)]=P[:,i*BS:(i+1)*BS].T
    l_ref[0:BS,blk(1)]=jnp.zeros((BS,BS),jnp.float32)
    top=wt_ref.shape[0]-2*BS
    wt_ref[top:top+BS,blk(0)]=WT[0]
    wt_ref[top+BS:,blk(0)]=jnp.zeros((BS,BS),jnp.float32)
    wt_ref[top:top+BS,blk(1)]=-dot3(dot3(WT[0],A[base:base+BS,base+BS:end],((1,),(0,))),WT[1],((1,),(0,)))
    wt_ref[top+BS:,blk(1)]=WT[1]
def pivot_one_kernel(ids_ref,hess_ref,*refs):
    srcs,(wt_ref,l_ref,u_ref,rest_ref,A,pk)=refs[:-6],refs[-6:]
    n=A.shape[0]; nblk=n//BS; half=n//2
    if len(srcs)==1: pk[...]=srcs[0][...]
    else:
        for m,src in enumerate(srcs):
            for c in range(2):
                unit=ids_ref[0]^(2*m+c)
                pk[pl.ds(pl.multiple_of(unit*UNIT,8),UNIT),:]=src[c*UNIT:(c+1)*UNIT,:]
    diag=lax.broadcasted_iota(jnp.int32,(BS,BS),0)==lax.broadcasted_iota(jnp.int32,(BS,BS),1)
    for (i,j),where in packed_places(nblk)[0].items():
        parts=[pk[row:row+high,lanes(g)] for _,row,g,high in where]
        v=parts[0] if len(parts)==1 else jnp.concatenate(parts,0)
        A[blk(i),blk(j)]=v+jnp.where(diag,hess_ref[:,blk(i)],0.0) if i==j else v
    panel_factor(A,wt_ref,l_ref,0)
    u=A[0:half,half:]
    u_ref[...]=u
    for k in range(half//BS):
        o=k*BS
        rest_ref[o:o+BS,o:]=A[half+o:half+o+BS,half+o:]-dot3(u[:,o:o+BS],u[:,o:],((0,),(0,)))
    rest_ref[BS:,0:BS]=jnp.zeros((BS,BS),jnp.float32)
def pivot_one(ids,hess,*srcs):
    n=hess.shape[0]; total=sum(s.shape[0] for s in srcs)
    sd=lambda r,c: jax.ShapeDtypeStruct((r,c),jnp.float32)
    vm=pl.BlockSpec(memory_space=pltpu.VMEM)
    return pl.pallas_call(pivot_one_kernel,out_shape=[sd(n//2,n//2),sd(n,n//2),sd(n//2,n//2),sd(n//2,n//2)],
        in_specs=[pl.BlockSpec(memory_space=pltpu.SMEM)]+[vm]*(1+len(srcs)),out_specs=[vm]*4,
        scratch_shapes=[pltpu.VMEM((n,n),jnp.float32),pltpu.VMEM((total,n),jnp.float32)],
        cost_estimate=pl.CostEstimate(flops=1,bytes_accessed=1,transcendentals=0),
        compiler_params=pltpu.CompilerParams(vmem_limit_bytes=16*2**20),name="pivot_one")(ids,hess[None],*srcs)
def own_rows(ids_ref,wt1_ref,wt2_ref,l1_ref,l2_ref,*refs):
    out_ref=refs[-1]
    @pl.when(ids_ref[0]==0)
    def _():
        out_ref[:,:PW]=l1_ref[...]
        out_ref[:PW,PW:]=jnp.zeros_like(l2_ref)
        out_ref[PW:,PW:]=l2_ref[...]
    @pl.when(ids_ref[0]>0)
    def _():
        rows=((0,),(0,))
        swap=ids_ref[1]>0
        per=len(refs)//2
        high=out_ref.shape[0]//per
        for part in range(per):
            mine,other=refs[2*part][...],refs[2*part+1][...]
            panel=jnp.concatenate([jnp.where(swap,other,mine),jnp.where(swap,mine,other)],0)
            to=slice(part*high,(part+1)*high)
            out_ref[to,:PW]=dot3(panel[:PW],wt1_ref[...],rows)
            out_ref[to,PW:]=dot3(panel,wt2_ref[...],rows)
def pivot_two_kernel(wt1_ref,u_ref,rest_ref,wt_ref,l_ref,A):
    half=wt1_ref.shape[0]
    A[...]=rest_ref[...]
    panel_factor(A,wt_ref,l_ref,0)
    wt_ref[0:half,:]=-dot3(wt1_ref[...],dot3(u_ref[...],wt_ref[half:,:],((1,),(0,))),((1,),(0,)))
def pivot_two(wt1,u,rest):
    half=wt1.shape[0]
    sd=lambda r,c: jax.ShapeDtypeStruct((r,c),jnp.float32)
    vm=pl.BlockSpec(memory_space=pltpu.VMEM)
    return pl.pallas_call(pivot_two_kernel,out_shape=[sd(2*half,half),sd(half,half)],
        in_specs=[vm]*3,out_specs=[vm]*2,scratch_shapes=[pltpu.VMEM((half,half),jnp.float32)],
        cost_estimate=pl.CostEstimate(flops=1,bytes_accessed=1,transcendentals=0),
        compiler_params=pltpu.CompilerParams(vmem_limit_bytes=16*2**20),name="pivot_two")(wt1,u,rest)


HOPS = {"x": ("scen", 2), "y": ("scen", 4), "z": ("grp", 1)}
ORDERS = ("xyz", "yzx", "zxy")


def flip(array, axis, mask):
    size = lax.axis_size(axis)
    return lax.ppermute(array, axis, [(i, i ^ mask) for i in range(size)])


def after(array, *others):
    return lax.optimization_barrier((array,) + others)[0]


def final_rows(ids, inverse, *halves):
    vmem = pl.BlockSpec(memory_space=pltpu.VMEM)
    return pl.pallas_call(
        own_rows,
        out_shape=jax.ShapeDtypeStruct((2 * HALF, 2 * PW), jnp.float32),
        in_specs=[pl.BlockSpec(memory_space=pltpu.SMEM)] + [vmem] * (4 + len(halves)),
        out_specs=vmem,
        compiler_params=pltpu.CompilerParams(vmem_limit_bytes=16 * 2**20),
        name="owned_rows",
    )(ids, *inverse, *halves)


def on_slice(coupling, scen_kkt, active_rows, first_hess):
    panel_cols = 2 * PW
    own = coupling.shape[2] // 8
    ids = jnp.stack([lax.axis_index("scen"), lax.axis_index("grp") % 2]).astype(jnp.int32)
    xt, packed, *away = scen_solve(ids, scen_kkt, coupling, active_rows, panel_cols, own)

    def blocks(pieces):
        return [piece.reshape((8,) + piece.shape[-2:]) for piece in pieces]

    got = [flip(piece, "scen", 1) for piece in blocks(away)]
    keeps = blocks(kept_products(ids, after(xt, *away), packed, coupling, own))

    sends, token = [], []
    for i in range(3):
        sends.append(keeps[i][4:] + after(got[i], *token)[4:])
        token = [sends[i]]
    fresh = [flip(sends[i], *HOPS[ORDERS[i][0]]) for i in range(3)]
    keeps = [keeps[i][:4] + after(got[i], *sends)[:4] for i in range(3)]
    got = fresh
    got[0] = after(got[0], *keeps)
    sends, token = [], []
    for i in range(3):
        sends.append(keeps[i][2:] + after(got[i], *token)[2:])
        token = [sends[i]]
    fresh = [flip(sends[i], *HOPS[ORDERS[i][1]]) for i in range(3)]
    keeps = [keeps[i][:2] + after(got[i], *sends)[:2] for i in range(3)]
    got = fresh
    got[0] = after(got[0], *keeps)
    main = CUTS[1]
    unit = jnp.concatenate(
        [
            keeps[0][0, main:] + got[0][0, main:],
            keeps[0][1, main : main + UNIT - FIRST] + got[0][1, main : main + UNIT - FIRST],
        ],
        0,
    )
    keeps[0], got[0] = keeps[0][:, :main], got[0][:, :main]
    sends, token = [jnp.concatenate([keeps[0][1] + got[0][1], unit], 0)], []
    for i in (1, 2):
        sends.append(keeps[i][1] + after(got[i], *sends)[1])
    fresh = [flip(sends[i], *HOPS[ORDERS[i][2]]) for i in range(3)]
    keeps = [keeps[i][0] + after(got[i], *sends)[0] for i in range(3)]
    unit = unit + after(fresh[0], *keeps)[main:]
    over_z = flip(unit, "grp", 2)
    unit = unit + after(over_z, unit)
    fresh = [after(f, unit) for f in fresh]
    slab = jnp.concatenate([keeps[0] + fresh[0][:main], keeps[1] + fresh[1], keeps[2] + fresh[2]], 0)
    got_far = flip(slab, "grp", 2)

    unit = after(unit, slab)
    pair = jnp.concatenate([unit, flip(unit, "scen", 1)], 0)
    pairs = [pair] + [flip(pair, "scen", 2 * m) for m in (1, 2, 3)]
    wt1, l1, u, left = pivot_one(ids, first_hess, *pairs)
    slab = slab + after(got_far, left)
    other = flip(slab, "grp", 1)
    wt2, l2 = pivot_two(wt1, u, after(left, slab))
    return final_rows(ids, (wt1, wt2, l1, l2), slab, after(other, wt2))


def any_mesh(coupling, scen_kkt, active_rows, first_hess):
    panel_cols = 2 * PW
    own_rows = coupling.shape[2] // lax.axis_size("scen")
    start = lax.axis_index("scen") * own_rows
    ids = jnp.zeros((2,), jnp.int32)
    xt, packed = scen_solve(ids, scen_kkt, coupling, active_rows, panel_cols)
    packed = lax.psum(packed, ("scen", "grp"))
    wt1, l1, u, left = pivot_one(ids, first_hess, packed)
    wt2, l2 = pivot_two(wt1, u, left)
    own = lax.psum_scatter(
        dot(xt, coupling[0], None), "scen", scatter_dimension=1, tiled=True
    )
    own = lax.psum(own, "grp")
    rows = jnp.concatenate([dotT(own[:PW], wt1), dotT(own, wt2)], 1)
    factor = jnp.concatenate([l1, jnp.concatenate([jnp.zeros_like(l2), l2], 0)], 1)
    padded = jnp.concatenate([factor, jnp.zeros((own_rows, panel_cols), jnp.float32)], 0)
    head = lax.dynamic_slice_in_dim(padded, jnp.minimum(start, panel_cols), own_rows)
    global_row = start + lax.broadcasted_iota(jnp.int32, (own_rows, 1), 0)
    return jnp.where(global_row < panel_cols, head, rows)


def solution(mesh):
    placed = (
        P(("scen", "grp"), None, None),
        P(("scen", "grp"), None, None),
        P(("scen", "grp")),
        P(),
    )
    whole = mesh.shape["scen"] == 8 and mesh.shape["grp"] == 4
    return jax.shard_map(
        on_slice if whole else any_mesh,
        mesh=mesh,
        in_specs=placed,
        out_specs=P("scen", None),
        check_vma=False,
    )
```

time: 138 us -> 125 us (0.906)
  the two profiles are of different devices: /device:TPU:6 before, /device:TPU:0 now
where the time goes in v3:
time: 125 us
  Pallas kernels  57.4 us (46%)
  waiting for transfers between devices  41 us (33%)
  starting transfers between devices  23.7 us (19%)
  other arithmetic  1.8 us (1%)
    ppermute x19, waiting for transfers between devices, flip(): return lax.ppermute(array, axis, [(i, i ^ mask) for i in range(size)])  41 us
    pallas_call x1, Pallas kernels, scen_solve(): pl.pallas_call(functools.partial(scen_kernel, away=bool(own)), out_shape=...  34 us
    ppermute x19, starting transfers between devices, flip(): return lax.ppermute(array, axis, [(i, i ^ mask) for i in range(size)])  23.7 us
    pallas_call x1, Pallas kernels, pivot_one(): pl.pallas_call(pivot_one_kernel, out_shape=[sd(n // 2, n // 2), sd(n, n /...  8.41 us
    pallas_call x1, Pallas kernels, pivot_two(): pl.pallas_call(pivot_two_kernel, out_shape=[sd(2 * half, half), sd(half,...  8.33 us
    pallas_call x1, Pallas kernels, kept_products(): pl.pallas_call(kept_kernel, out_shape=outs, in_specs=[smem, vmem, vmem, a...  5.08 us
  transfers between devices with their start and end apart: 19, of which 10 were waited for; matrix products, arithmetic and copies ran while one was open for 2% of the time, Pallas kernels for 17%

profile of v3, /device:TPU:0, one launch (start us, length us, event | category | flops | bytes accessed | tf_op | source)
XLA Modules:
  0.0 125.3 jit_solution(9606917978943143741)
XLA Ops:
  0.7 0.1 pad_add_fusion.ids_ref
  0.7 34.0 %scen_solve.1 = (bf16[512,768]{1,0:T(8,128)(2,1)S(1)}, f32[320,512]{1,0:T(8,128)S(1)}, f32[2,2,2,96,512]{4,3,2,1,0:T(8,128)}, f32[2,2,2,96,512]{4,3,2,1,0:T(8,128)}, f32[2,2,2,88,512]{4,3,2,1,0:T(8,128)}) custom-call(s32[2]{0:T(128)S(1)} %pad_add_fusion.ids_ref, s32[1]{0:T(128)S(6)} %copy.6.act_ref, bf16[1,768,768]{2,1,0:T(8,128)(2,1)} %k_ref.1, ...), custom_call_target="tpu_custom_call" | custom-call | tf_op jit(solution)/shard_map/scen_solve/pallas_call | solution.py:216
  34.8 0.5 collective-permute-start
  35.3 0.1 collective-permute-start.1
  35.4 0.4 collective-permute-start.2
  35.8 5.1 %kept_products.1 = (f32[2,2,2,96,512]{4,3,2,1,0:T(8,128)S(1)}, f32[2,2,2,96,512]{4,3,2,1,0:T(8,128)S(1)}, f32[2,2,2,88,512]{4,3,2,1,0:T(8,128)S(1)}) custom-call(s32[2]{0:T(128)S(1)} %pad_add_fusion.ids_ref, bf16[512,768]{1,0:T(8,128)(2,1)S(1)} %get-tuple-element.50.xt_ref, f32[320,512]{1,0:T(8,128)S(1)} %get-tuple-element.51.packed_ref, ...), custom_call_target="tpu_custom_call" | custom-call | flops 1610612736 | bytes 11534336 | tf_op jit(solution)/shard_map/kept_products/pallas_call | solution.py:230
  40.9 0.1 fusion.11
  41.0 0.1 fusion.10
  41.1 0.1 fusion.9
  41.3 0.2 slice_add_fusion
  41.5 2.6 %collective-permute-start.3 = (f32[4,96,512]{2,1,0:T(8,128)S(1)}, f32[4,96,512]{2,1,0:T(8,128)S(1)}, u32[]{:S(2)}, u32[]{:S(2)}) collective-permute-start(f32[4,96,512]{2,1,0:T(8,128)S(1)} %slice_add_fusion), channel_id=1, source_target_pairs={{0,8},{4,12},{8,0},{12,4},{16,24},{20,28},{24,16},{28,20},{1,9},{5... | collective-permute-start | bytes 2359304 | tf_op jit(solution)/shard_map/ppermute | solution.py:327
  44.1 0.2 bitcast_add_fusion.1
  44.3 1.6 %collective-permute-start.4 = (f32[4,96,512]{2,1,0:T(8,128)S(1)}, f32[4,96,512]{2,1,0:T(8,128)S(1)}, u32[]{:S(2)}, u32[]{:S(2)}) collective-permute-start(f32[4,96,512]{2,1,0:T(8,128)S(1)} %bitcast_add_fusion.1), channel_id=1, source_target_pairs={{0,16},{4,20},{8,24},{12,28},{16,0},{20,4},{24,8},{28,12},{1,17},{... | collective-permute-start | bytes 2359304 | tf_op jit(solution)/shard_map/ppermute | solution.py:327
  45.8 0.1 bitcast_add_fusion.4
  46.0 1.6 %collective-permute-start.5 = (f32[4,88,512]{2,1,0:T(8,128)S(1)}, f32[4,88,512]{2,1,0:T(8,128)S(1)}, u32[]{:S(2)}, u32[]{:S(2)}) collective-permute-start(f32[4,88,512]{2,1,0:T(8,128)S(1)} %bitcast_add_fusion.4), channel_id=1, source_target_pairs={{0,1},{1,0},{2,3},{3,2},{4,5},{5,4},{6,7},{7,6},{8,9},{9,8},{10,11... | collective-permute-start | bytes 2162696 | tf_op jit(solution)/shard_map/ppermute | solution.py:327
  47.6 0.4 bitcast_add_fusion
  48.0 0.2 bitcast_add_fusion.3
  48.2 14.1 %collective-permute-done.3 = f32[4,96,512]{2,1,0:T(8,128)S(1)} collective-permute-done((f32[4,96,512]{2,1,0:T(8,128)S(1)}, f32[4,96,512]{2,1,0:T(8,128)S(1)}, u32[]{:S(2)}, u32[]{:S(2)}) %collective-permute-start.3) | collective-permute-done | bytes 786464 | tf_op jit(solution)/shard_map/ppermute | solution.py:327
  62.2 0.1 slice_add_fusion.3
  62.3 1.8 %collective-permute-start.6 = (f32[2,96,512]{2,1,0:T(8,128)S(1)}, f32[2,96,512]{2,1,0:T(8,128)S(1)}, u32[]{:S(2)}, u32[]{:S(2)}) collective-permute-start(f32[2,96,512]{2,1,0:T(8,128)S(1)} %slice_add_fusion.3), channel_id=1, source_target_pairs={{0,16},{4,20},{8,24},{12,28},{16,0},{20,4},{24,8},{28,12},{1,17},{... | collective-permute-start | bytes 1179656 | tf_op jit(solution)/shard_map/ppermute | solution.py:327
  64.2 0.1 slice_add_fusion.2
  64.2 1.6 %collective-permute-start.8 = (f32[2,96,512]{2,1,0:T(8,128)S(1)}, f32[2,96,512]{2,1,0:T(8,128)S(1)}, u32[]{:S(2)}, u32[]{:S(2)}) collective-permute-start(f32[2,96,512]{2,1,0:T(8,128)S(1)} %slice_add_fusion.2), channel_id=1, source_target_pairs={{0,1},{1,0},{2,3},{3,2},{4,5},{5,4},{6,7},{7,6},{8,9},{9,8},{10,11... | collective-permute-start | bytes 1179656 | tf_op jit(solution)/shard_map/ppermute | solution.py:327
  65.9 1.6 %collective-permute-start.9 = (f32[2,88,512]{2,1,0:T(8,128)S(1)}, f32[2,88,512]{2,1,0:T(8,128)S(1)}, u32[]{:S(2)}, u32[]{:S(2)}) collective-permute-start(f32[2,88,512]{2,1,0:T(8,128)S(1)} %slice_add_fusion.6), channel_id=1, source_target_pairs={{0,8},{4,12},{8,0},{12,4},{16,24},{20,28},{24,16},{28,20},{1,9},{5... | collective-permute-start | bytes 1081352 | tf_op jit(solution)/shard_map/ppermute | solution.py:327
  67.5 0.1 slice_add_fusion.1
  67.5 0.1 slice_add_fusion.5
  67.6 0.1 slice_add_fusion.4
  67.7 5.6 %collective-permute-done.6 = f32[2,96,512]{2,1,0:T(8,128)S(1)} collective-permute-done((f32[2,96,512]{2,1,0:T(8,128)S(1)}, f32[2,96,512]{2,1,0:T(8,128)S(1)}, u32[]{:S(2)}, u32[]{:S(2)}) %collective-permute-start.6) | collective-permute-done | bytes 393248 | tf_op jit(solution)/shard_map/ppermute | solution.py:327
  73.4 1.7 %collective-permute-start.7 = (f32[112,512]{1,0:T(8,128)S(1)}, f32[112,512]{1,0:T(8,128)S(1)}, u32[]{:S(2)}, u32[]{:S(2)}) collective-permute-start(f32[112,512]{1,0:T(8,128)S(1)} %pad_maximum_fusion.1), channel_id=1, source_target_pairs={{0,1},{1,0},{2,3},{3,2},{4,5},{5,4},{6,7},{7,6},{8,9},{9,8},{10,11... | collective-permute-start | bytes 688136 | tf_op jit(solution)/shard_map/ppermute | solution.py:327
  75.1 1.6 %collective-permute-start.11 = (f32[96,512]{1,0:T(8,128)S(1)}, f32[96,512]{1,0:T(8,128)S(1)}, u32[]{:S(2)}, u32[]{:S(2)}) collective-permute-start(f32[96,512]{1,0:T(8,128)S(1)} %fusion.1), channel_id=1, source_target_pairs={{0,8},{4,12},{8,0},{12,4},{16,24},{20,28},{24,16},{28,20},{1,9},{5... | collective-permute-start | bytes 589832 | tf_op jit(solution)/shard_map/ppermute | solution.py:327
  76.8 3.1 %collective-permute-done.7 = f32[112,512]{1,0:T(8,128)S(1)} collective-permute-done((f32[112,512]{1,0:T(8,128)S(1)}, f32[112,512]{1,0:T(8,128)S(1)}, u32[]{:S(2)}, u32[]{:S(2)}) %collective-permute-start.7) | collective-permute-done | bytes 229408 | tf_op jit(solution)/shard_map/ppermute | solution.py:327
  79.9 2.5 %collective-permute-start.10 = (f32[40,512]{1,0:T(8,128)S(1)}, f32[40,512]{1,0:T(8,128)S(1)}, u32[]{:S(2)}, u32[]{:S(2)}) collective-permute-start(f32[40,512]{1,0:T(8,128)S(1)} %maximum_add_fusion), channel_id=1, source_target_pairs={{0,2},{1,3},{2,0},{3,1},{4,6},{5,7},{6,4},{7,5},{8,10},{9,11},{10,... | collective-permute-start | bytes 245768 | tf_op jit(solution)/shard_map/ppermute | solution.py:327
  82.4 1.5 %collective-permute-start.12 = (f32[88,512]{1,0:T(8,128)S(1)}, f32[88,512]{1,0:T(8,128)S(1)}, u32[]{:S(2)}, u32[]{:S(2)}) collective-permute-start(f32[88,512]{1,0:T(8,128)S(1)} %fusion.3), channel_id=1, source_target_pairs={{0,16},{4,20},{8,24},{12,28},{16,0},{20,4},{24,8},{28,12},{1,17},{... | collective-permute-start | bytes 540680 | tf_op jit(solution)/shard_map/ppermute | solution.py:327
  84.0 1.4 %collective-permute-done.10 = f32[40,512]{1,0:T(8,128)S(1)} collective-permute-done((f32[40,512]{1,0:T(8,128)S(1)}, f32[40,512]{1,0:T(8,128)S(1)}, u32[]{:S(2)}, u32[]{:S(2)}) %collective-permute-start.10) | collective-permute-done | bytes 81952 | tf_op jit(solution)/shard_map/ppermute | solution.py:327
  85.5 2.5 %collective-permute-done.12 = f32[88,512]{1,0:T(8,128)S(1)} collective-permute-done((f32[88,512]{1,0:T(8,128)S(1)}, f32[88,512]{1,0:T(8,128)S(1)}, u32[]{:S(2)}, u32[]{:S(2)}) %collective-permute-start.12) | collective-permute-done | bytes 180256 | tf_op jit(solution)/shard_map/ppermute | solution.py:327
  88.0 0.6 collective-permute-start.17
  88.6 1.3 %collective-permute-done.13 = f32[40,512]{1,0:T(8,128)S(1)} collective-permute-done((f32[40,512]{1,0:T(8,128)S(1)}, f32[40,512]{1,0:T(8,128)S(1)}, u32[]{:S(2)}, u32[]{:S(2)}) %collective-permute-start.13) | collective-permute-done | bytes 81952 | tf_op jit(solution)/shard_map/ppermute | solution.py:327
  89.9 1.4 %collective-permute-start.14 = (f32[80,512]{1,0:T(8,128)S(1)}, f32[80,512]{1,0:T(8,128)S(1)}, u32[]{:S(2)}, u32[]{:S(2)}) collective-permute-start(f32[80,512]{1,0:T(8,128)S(1)} %constant_dynamic-update-slice_fusion.refs_0_), channel_id=1, source_target_pairs={{0,8},{4,12},{8,0},{12,4},{16,24},{20,28},{24,16},{28,20},{1,9},{5... | collective-permute-start | bytes 491528 | tf_op jit(solution)/shard_map/ppermute | solution.py:327
  91.3 1.5 %collective-permute-start.15 = (f32[80,512]{1,0:T(8,128)S(1)}, f32[80,512]{1,0:T(8,128)S(1)}, u32[]{:S(2)}, u32[]{:S(2)}) collective-permute-start(f32[80,512]{1,0:T(8,128)S(1)} %constant_dynamic-update-slice_fusion.refs_0_), channel_id=1, source_target_pairs={{0,16},{4,20},{8,24},{12,28},{16,0},{20,4},{24,8},{28,12},{1,17},{... | collective-permute-start | bytes 491528 | tf_op jit(solution)/shard_map/ppermute | solution.py:327
  92.8 0.6 collective-permute-start.16
  93.4 3.6 %collective-permute-done.14.refs_1_ = f32[80,512]{1,0:T(8,128)S(1)} collective-permute-done((f32[80,512]{1,0:T(8,128)S(1)}, f32[80,512]{1,0:T(8,128)S(1)}, u32[]{:S(2)}, u32[]{:S(2)}) %collective-permute-start.14) | collective-permute-done | bytes 163872 | tf_op jit(solution)/shard_map/ppermute | solution.py:327
  97.0 3.7 %collective-permute-done.15.refs_2_ = f32[80,512]{1,0:T(8,128)S(1)} collective-permute-done((f32[80,512]{1,0:T(8,128)S(1)}, f32[80,512]{1,0:T(8,128)S(1)}, u32[]{:S(2)}, u32[]{:S(2)}) %collective-permute-start.15) | collective-permute-done | bytes 163872 | tf_op jit(solution)/shard_map/ppermute | solution.py:327
  100.7 8.4 %pivot_one.1 = (f32[256,256]{1,0:T(8,128)S(1)}, f32[512,256]{1,0:T(8,128)S(1)}, f32[256,256]{1,0:T(8,128)S(1)}, f32[256,256]{1,0:T(8,128)S(1)}) custom-call(s32[2]{0:T(128)S(1)} %pad_add_fusion.ids_ref, f32[1,512]{1,0:T(1,128)S(1)} %bitcast.34, f32[80,512]{1,0:T(8,128)S(1)} %constant_dynamic-update-slice_fusion.refs_0_, ...), custom_call_target="tpu_custom_call" | custom-call | flops 1 | bytes 1 | tf_op jit(solution)/shard_map/pivot_one/pallas_call | solution.py:282
  109.1 1.6 %collective-permute-done.17 = f32[256,512]{1,0:T(8,128)S(1)} collective-permute-done((f32[256,512]{1,0:T(8,128)S(1)}, f32[256,512]{1,0:T(8,128)S(1)}, u32[]{:S(2)}, u32[]{:S(2)}) %collective-permute-start.17) | collective-permute-done | bytes 524320 | tf_op jit(solution)/shard_map/ppermute | solution.py:327
  110.7 0.1 fusion.8.refs_0_
  110.8 0.4 collective-permute-start.18
  111.2 8.3 %pivot_two.1 = (f32[512,256]{1,0:T(8,128)S(1)}, f32[256,256]{1,0:T(8,128)S(1)}) custom-call(f32[256,256]{1,0:T(8,128)S(1)} %get-tuple-element.78.wt1_ref, f32[256,256]{1,0:T(8,128)S(1)} %get-tuple-element.79.u_ref, f32[256,256]{1,0:T(8,128)S(1)} %get-tuple-element.82.rest_ref), custom_call_target="tpu_custom_call" | custom-call | flops 1 | bytes 1 | tf_op jit(solution)/shard_map/pivot_two/pallas_call | solution.py:315
  119.6 4.1 %collective-permute-done.18.refs_1_ = f32[256,512]{1,0:T(8,128)S(1)} collective-permute-done((f32[256,512]{1,0:T(8,128)S(1)}, f32[256,512]{1,0:T(8,128)S(1)}, u32[]{:S(2)}, u32[]{:S(2)}) %collective-permute-start.18) | collective-permute-done | bytes 524320 | tf_op jit(solution)/shard_map/ppermute | solution.py:327
  123.7 1.6 %owned_rows.1 = f32[512,512]{1,0:T(8,128)} custom-call(s32[2]{0:T(128)S(1)} %pad_add_fusion.ids_ref, f32[256,256]{1,0:T(8,128)S(1)} %get-tuple-element.78.wt1_ref, f32[512,256]{1,0:T(8,128)S(1)} %get-tuple-element.83.wt2_ref, f32[512,256]{1,0:T(8,128)S(1)} %get-tuple-element.84.l1_ref, f32[256,256]{1,0:T(8,128)S(1)} %get-tuple-element.85.l2_ref, ...), custom_call_target="tpu_custom_call" | custom-call | tf_op jit(solution)/shard_map/owned_rows/pallas_call | solution.py:336
  (33 shorter events, 0.5 us)
Async XLA Ops:
  0.7 35.1 %copy-start = (bf16[1,768,4096]{2,1,0:T(8,128)(2,1)S(1)}, bf16[1,768,4096]{2,1,0:T(8,128)(2,1)}, u32[]{:S(2)}) copy-start(bf16[1,768,4096]{2,1,0:T(8,128)(2,1)} %c_hbm.3) | copy-start | bytes 18874372
  34.8 6.5 %collective-permute-start = (f32[8,96,512]{2,1,0:T(8,128)}, f32[8,96,512]{2,1,0:T(8,128)S(1)}, u32[]{:S(2)}, u32[]{:S(2)}) collective-permute-start(f32[8,96,512]{2,1,0:T(8,128)} %bitcast.36), channel_id=1, source_target_pairs={{0,4},{4,0},{8,12},{12,8},{16,20},{20,16},{24,28},{28,24},{1,5},{5... | collective-permute-start | bytes 4718600 | tf_op jit(solution)/shard_map/ppermute | solution.py:327
  35.3 8.8 %collective-permute-start.1 = (f32[8,96,512]{2,1,0:T(8,128)}, f32[8,96,512]{2,1,0:T(8,128)S(1)}, u32[]{:S(2)}, u32[]{:S(2)}) collective-permute-start(f32[8,96,512]{2,1,0:T(8,128)} %bitcast.35), channel_id=1, source_target_pairs={{0,4},{4,0},{8,12},{12,8},{16,20},{20,16},{24,28},{28,24},{1,5},{5... | collective-permute-start | bytes 4718600 | tf_op jit(solution)/shard_map/ppermute | solution.py:327
  35.4 10.5 %collective-permute-start.2 = (f32[8,88,512]{2,1,0:T(8,128)}, f32[8,88,512]{2,1,0:T(8,128)S(1)}, u32[]{:S(2)}, u32[]{:S(2)}) collective-permute-start(f32[8,88,512]{2,1,0:T(8,128)} %bitcast.37), channel_id=1, source_target_pairs={{0,4},{4,0},{8,12},{12,8},{16,20},{20,16},{24,28},{28,24},{1,5},{5... | collective-permute-start | bytes 4325384 | tf_op jit(solution)/shard_map/ppermute | solution.py:327
  41.5 20.8 %collective-permute-start.3 = (f32[4,96,512]{2,1,0:T(8,128)S(1)}, f32[4,96,512]{2,1,0:T(8,128)S(1)}, u32[]{:S(2)}, u32[]{:S(2)}) collective-permute-start(f32[4,96,512]{2,1,0:T(8,128)S(1)} %slice_add_fusion), channel_id=1, source_target_pairs={{0,8},{4,12},{8,0},{12,4},{16,24},{20,28},{24,16},{28,20},{1,9},{5... | collective-permute-start | bytes 2359304 | tf_op jit(solution)/shard_map/ppermute | solution.py:327
  44.3 19.9 %collective-permute-start.4 = (f32[4,96,512]{2,1,0:T(8,128)S(1)}, f32[4,96,512]{2,1,0:T(8,128)S(1)}, u32[]{:S(2)}, u32[]{:S(2)}) collective-permute-start(f32[4,96,512]{2,1,0:T(8,128)S(1)} %bitcast_add_fusion.1), channel_id=1, source_target_pairs={{0,16},{4,20},{8,24},{12,28},{16,0},{20,4},{24,8},{28,12},{1,17},{... | collective-permute-start | bytes 2359304 | tf_op jit(solution)/shard_map/ppermute | solution.py:327
  46.0 19.9 %collective-permute-start.5 = (f32[4,88,512]{2,1,0:T(8,128)S(1)}, f32[4,88,512]{2,1,0:T(8,128)S(1)}, u32[]{:S(2)}, u32[]{:S(2)}) collective-permute-start(f32[4,88,512]{2,1,0:T(8,128)S(1)} %bitcast_add_fusion.4), channel_id=1, source_target_pairs={{0,1},{1,0},{2,3},{3,2},{4,5},{5,4},{6,7},{7,6},{8,9},{9,8},{10,11... | collective-permute-start | bytes 2162696 | tf_op jit(solution)/shard_map/ppermute | solution.py:327
  62.3 10.9 %collective-permute-start.6 = (f32[2,96,512]{2,1,0:T(8,128)S(1)}, f32[2,96,512]{2,1,0:T(8,128)S(1)}, u32[]{:S(2)}, u32[]{:S(2)}) collective-permute-start(f32[2,96,512]{2,1,0:T(8,128)S(1)} %slice_add_fusion.3), channel_id=1, source_target_pairs={{0,16},{4,20},{8,24},{12,28},{16,0},{20,4},{24,8},{28,12},{1,17},{... | collective-permute-start | bytes 1179656 | tf_op jit(solution)/shard_map/ppermute | solution.py:327
  64.2 10.8 %collective-permute-start.8 = (f32[2,96,512]{2,1,0:T(8,128)S(1)}, f32[2,96,512]{2,1,0:T(8,128)S(1)}, u32[]{:S(2)}, u32[]{:S(2)}) collective-permute-start(f32[2,96,512]{2,1,0:T(8,128)S(1)} %slice_add_fusion.2), channel_id=1, source_target_pairs={{0,1},{1,0},{2,3},{3,2},{4,5},{5,4},{6,7},{7,6},{8,9},{9,8},{10,11... | collective-permute-start | bytes 1179656 | tf_op jit(solution)/shard_map/ppermute | solution.py:327
  65.9 10.7 %collective-permute-start.9 = (f32[2,88,512]{2,1,0:T(8,128)S(1)}, f32[2,88,512]{2,1,0:T(8,128)S(1)}, u32[]{:S(2)}, u32[]{:S(2)}) collective-permute-start(f32[2,88,512]{2,1,0:T(8,128)S(1)} %slice_add_fusion.6), channel_id=1, source_target_pairs={{0,8},{4,12},{8,0},{12,4},{16,24},{20,28},{24,16},{28,20},{1,9},{5... | collective-permute-start | bytes 1081352 | tf_op jit(solution)/shard_map/ppermute | solution.py:327
  73.4 6.6 %collective-permute-start.7 = (f32[112,512]{1,0:T(8,128)S(1)}, f32[112,512]{1,0:T(8,128)S(1)}, u32[]{:S(2)}, u32[]{:S(2)}) collective-permute-start(f32[112,512]{1,0:T(8,128)S(1)} %pad_maximum_fusion.1), channel_id=1, source_target_pairs={{0,1},{1,0},{2,3},{3,2},{4,5},{5,4},{6,7},{7,6},{8,9},{9,8},{10,11... | collective-permute-start | bytes 688136 | tf_op jit(solution)/shard_map/ppermute | solution.py:327
  75.1 10.3 %collective-permute-start.11 = (f32[96,512]{1,0:T(8,128)S(1)}, f32[96,512]{1,0:T(8,128)S(1)}, u32[]{:S(2)}, u32[]{:S(2)}) collective-permute-start(f32[96,512]{1,0:T(8,128)S(1)} %fusion.1), channel_id=1, source_target_pairs={{0,8},{4,12},{8,0},{12,4},{16,24},{20,28},{24,16},{28,20},{1,9},{5... | collective-permute-start | bytes 589832 | tf_op jit(solution)/shard_map/ppermute | solution.py:327
  79.9 20.8 %copy-start.1 = (f32[512]{0:T(512)S(1)}, f32[512]{0:T(512)}, u32[]{:S(2)}) copy-start(f32[512]{0:T(512)} %param.7) | copy-start | bytes 6148
  79.9 5.4 %collective-permute-start.10 = (f32[40,512]{1,0:T(8,128)S(1)}, f32[40,512]{1,0:T(8,128)S(1)}, u32[]{:S(2)}, u32[]{:S(2)}) collective-permute-start(f32[40,512]{1,0:T(8,128)S(1)} %maximum_add_fusion), channel_id=1, source_target_pairs={{0,2},{1,3},{2,0},{3,1},{4,6},{5,7},{6,4},{7,5},{8,10},{9,11},{10,... | collective-permute-start | bytes 245768 | tf_op jit(solution)/shard_map/ppermute | solution.py:327
  82.4 5.5 %collective-permute-start.12 = (f32[88,512]{1,0:T(8,128)S(1)}, f32[88,512]{1,0:T(8,128)S(1)}, u32[]{:S(2)}, u32[]{:S(2)}) collective-permute-start(f32[88,512]{1,0:T(8,128)S(1)} %fusion.3), channel_id=1, source_target_pairs={{0,16},{4,20},{8,24},{12,28},{16,0},{20,4},{24,8},{28,12},{1,17},{... | collective-permute-start | bytes 540680 | tf_op jit(solution)/shard_map/ppermute | solution.py:327
  88.0 22.7 %collective-permute-start.17 = (f32[256,512]{1,0:T(8,128)S(1)}, f32[256,512]{1,0:T(8,128)S(1)}, u32[]{:S(2)}, u32[]{:S(2)}) collective-permute-start(f32[256,512]{1,0:T(8,128)S(1)} %pad_maximum_fusion), channel_id=1, source_target_pairs={{0,2},{1,3},{2,0},{3,1},{4,6},{5,7},{6,4},{7,5},{8,10},{9,11},{10,... | collective-permute-start | bytes 1572872 | tf_op jit(solution)/shard_map/ppermute | solution.py:327
  88.6 1.3 %collective-permute-start.13 = (f32[40,512]{1,0:T(8,128)S(1)}, f32[40,512]{1,0:T(8,128)S(1)}, u32[]{:S(2)}, u32[]{:S(2)}) collective-permute-start(f32[40,512]{1,0:T(8,128)S(1)} %add.136), channel_id=1, source_target_pairs={{0,4},{4,0},{8,12},{12,8},{16,20},{20,16},{24,28},{28,24},{1,5},{5... | collective-permute-start | bytes 245768 | tf_op jit(solution)/shard_map/ppermute | solution.py:327
  89.9 7.1 %collective-permute-start.14 = (f32[80,512]{1,0:T(8,128)S(1)}, f32[80,512]{1,0:T(8,128)S(1)}, u32[]{:S(2)}, u32[]{:S(2)}) collective-permute-start(f32[80,512]{1,0:T(8,128)S(1)} %constant_dynamic-update-slice_fusion.refs_0_), channel_id=1, source_target_pairs={{0,8},{4,12},{8,0},{12,4},{16,24},{20,28},{24,16},{28,20},{1,9},{5... | collective-permute-start | bytes 491528 | tf_op jit(solution)/shard_map/ppermute | solution.py:327
  91.3 9.4 %collective-permute-start.15 = (f32[80,512]{1,0:T(8,128)S(1)}, f32[80,512]{1,0:T(8,128)S(1)}, u32[]{:S(2)}, u32[]{:S(2)}) collective-permute-start(f32[80,512]{1,0:T(8,128)S(1)} %constant_dynamic-update-slice_fusion.refs_0_), channel_id=1, source_target_pairs={{0,16},{4,20},{8,24},{12,28},{16,0},{20,4},{24,8},{28,12},{1,17},{... | collective-permute-start | bytes 491528 | tf_op jit(solution)/shard_map/ppermute | solution.py:327
  92.8 7.9 %collective-permute-start.16 = (f32[80,512]{1,0:T(8,128)S(1)}, f32[80,512]{1,0:T(8,128)S(1)}, u32[]{:S(2)}, u32[]{:S(2)}) collective-permute-start(f32[80,512]{1,0:T(8,128)S(1)} %constant_dynamic-update-slice_fusion.refs_0_), channel_id=1, source_target_pairs={{0,24},{4,28},{8,16},{12,20},{16,8},{20,12},{24,0},{28,4},{1,25},{... | collective-permute-start | bytes 491528 | tf_op jit(solution)/shard_map/ppermute | solution.py:327
  110.8 12.8 %collective-permute-start.18 = (f32[256,512]{1,0:T(8,128)S(1)}, f32[256,512]{1,0:T(8,128)S(1)}, u32[]{:S(2)}, u32[]{:S(2)}) collective-permute-start(f32[256,512]{1,0:T(8,128)S(1)} %fusion.8.refs_0_), channel_id=1, source_target_pairs={{0,1},{1,0},{2,3},{3,2},{4,5},{5,4},{6,7},{7,6},{8,9},{9,8},{10,11... | collective-permute-start | bytes 1572872 | tf_op jit(solution)/shard_map/ppermute | solution.py:327

commit v4 on v3

--- a/solution.py
+++ b/solution.py
@@ -190,13 +190,21 @@
         Wk[...]=W
         return 0
     lax.fori_loop(0,nblk,step,0)
-    for part in sweep(nblk-1,True): part()
+    invert,scale=sweep(nblk-1,True)[:2]
+    invert()
+    last=blk(nblk-1)
+    left[last,0:BS]=(-eye).astype(jnp.bfloat16)
     fetch.wait()
     panel=panel_ref[...]
     kept=lax.broadcasted_iota(jnp.int32,(n,1),0)<act_ref[0]
     masked=jnp.where(kept,panel,jnp.zeros((),jnp.bfloat16))
-    hi,lo=halves(M[...])
-    x=dotT(masked,hi,None)+dotT(masked,lo,None)
+    hi,lo=halves(M[0:n-BS,:])
+    x=dotT(masked[0:n-BS],hi,None)+dotT(masked[0:n-BS],lo,None)
+    scale()
+    spread=dotT(masked,left[:,0:BS],None)+dotT(masked,left[:,2*BS:],None)
+    hi,lo=halves(spread)
+    x=x-dot(jnp.concatenate([hi,hi,lo],1),right[...],None)
+    x=x-jnp.concatenate([jnp.zeros((x.shape[0],n-BS),jnp.float32),masked[last].astype(jnp.float32).T],1)
     kept=lax.broadcasted_iota(jnp.int32,(1,n),1)<act_ref[0]
     x=jnp.where(kept,-x,0.0).astype(jnp.bfloat16)
     x_ref[...]=x
@@ -284,25 +292,28 @@
         scratch_shapes=[pltpu.VMEM((n,n),jnp.float32),pltpu.VMEM((total,n),jnp.float32)],
         cost_estimate=pl.CostEstimate(flops=1,bytes_accessed=1,transcendentals=0),
         compiler_params=pltpu.CompilerParams(vmem_limit_bytes=16*2**20),name="pivot_one")(ids,hess[None],*srcs)
-def own_rows(ids_ref,wt1_ref,wt2_ref,l1_ref,l2_ref,*refs):
-    out_ref=refs[-1]
+def half_rows(wt1_ref,wt2_ref,panel,out_ref,first,held):
+    rows=((0,),(0,))
+    @pl.when(first)
+    def _():
+        left,right=dot3(panel,wt1_ref[...],rows),dot3(panel,wt2_ref[:PW],rows)
+        out_ref[:,:PW]=left if held is None else held[:,:PW]+left
+        out_ref[:,PW:]=right if held is None else held[:,PW:]+right
+    @pl.when(jnp.logical_not(first))
+    def _():
+        right=dot3(panel,wt2_ref[PW:],rows)
+        out_ref[:,:PW]=jnp.zeros_like(right) if held is None else held[:,:PW]
+        out_ref[:,PW:]=right if held is None else held[:,PW:]+right
+def mine_rows(ids_ref,wt1_ref,wt2_ref,mine_ref,out_ref):
+    half_rows(wt1_ref,wt2_ref,mine_ref[...],out_ref,ids_ref[1]==0,None)
+def own_rows(ids_ref,wt1_ref,wt2_ref,l1_ref,l2_ref,held_ref,other_ref,out_ref):
     @pl.when(ids_ref[0]==0)
     def _():
         out_ref[:,:PW]=l1_ref[...]
         out_ref[:PW,PW:]=jnp.zeros_like(l2_ref)
         out_ref[PW:,PW:]=l2_ref[...]
     @pl.when(ids_ref[0]>0)
-    def _():
-        rows=((0,),(0,))
-        swap=ids_ref[1]>0
-        per=len(refs)//2
-        high=out_ref.shape[0]//per
-        for part in range(per):
-            mine,other=refs[2*part][...],refs[2*part+1][...]
-            panel=jnp.concatenate([jnp.where(swap,other,mine),jnp.where(swap,mine,other)],0)
-            to=slice(part*high,(part+1)*high)
-            out_ref[to,:PW]=dot3(panel[:PW],wt1_ref[...],rows)
-            out_ref[to,PW:]=dot3(panel,wt2_ref[...],rows)
+    def _(): half_rows(wt1_ref,wt2_ref,other_ref[...],out_ref,ids_ref[1]>0,held_ref)
 def pivot_two_kernel(wt1_ref,u_ref,rest_ref,wt_ref,l_ref,A):
     half=wt1_ref.shape[0]
     A[...]=rest_ref[...]
@@ -331,16 +342,17 @@
     return lax.optimization_barrier((array,) + others)[0]
 
 
-def final_rows(ids, inverse, *halves):
+def final_rows(kernel, ids, *args):
     vmem = pl.BlockSpec(memory_space=pltpu.VMEM)
     return pl.pallas_call(
-        own_rows,
+        kernel,
         out_shape=jax.ShapeDtypeStruct((2 * HALF, 2 * PW), jnp.float32),
-        in_specs=[pl.BlockSpec(memory_space=pltpu.SMEM)] + [vmem] * (4 + len(halves)),
+        in_specs=[pl.BlockSpec(memory_space=pltpu.SMEM)] + [vmem] * len(args),
         out_specs=vmem,
+        cost_estimate=pl.CostEstimate(flops=1, bytes_accessed=1, transcendentals=0),
         compiler_params=pltpu.CompilerParams(vmem_limit_bytes=16 * 2**20),
         name="owned_rows",
-    )(ids, *inverse, *halves)
+    )(ids, *args)
 
 
 def on_slice(coupling, scen_kkt, active_rows, first_hess):
@@ -399,7 +411,8 @@
     slab = slab + after(got_far, left)
     other = flip(slab, "grp", 1)
     wt2, l2 = pivot_two(wt1, u, after(left, slab))
-    return final_rows(ids, (wt1, wt2, l1, l2), slab, after(other, wt2))
+    held = final_rows(mine_rows, ids, wt1, wt2, slab)
+    return final_rows(own_rows, ids, wt1, wt2, l1, l2, held, after(other, held))
 
 
 def any_mesh(coupling, scen_kkt, active_rows, first_hess):

time: 125 us -> 125 us (level)
  waiting for transfers between devices: 41 us -> 39.7 us
    pallas_call x1 -> x2, Pallas kernels: 1.59 us -> 2.8 us  [final_rows(): pl.pallas_call(kernel, out_shape=jax.ShapeDtypeStruct((2 * HALF, 2 * PW),...]
  transfers between devices with their start and end apart: 19 -> 19, of which waited for: 10 -> 10; matrix products, arithmetic and copies ran while one was open for 2% -> 2% of each run, Pallas kernels for 17% -> 18%
where the time goes in v4:
time: 125 us
  Pallas kernels  58.3 us (47%)
  waiting for transfers between devices  39.7 us (32%)
  starting transfers between devices  23.7 us (19%)
  other arithmetic  1.79 us (1%)
    ppermute x19, waiting for transfers between devices, flip(): return lax.ppermute(array, axis, [(i, i ^ mask) for i in range(size)])  39.7 us
    pallas_call x1, Pallas kernels, scen_solve(): pl.pallas_call(functools.partial(scen_kernel, away=bool(own)), out_shape=...  33.6 us
    ppermute x19, starting transfers between devices, flip(): return lax.ppermute(array, axis, [(i, i ^ mask) for i in range(size)])  23.7 us
    pallas_call x1, Pallas kernels, pivot_one(): pl.pallas_call(pivot_one_kernel, out_shape=[sd(n // 2, n // 2), sd(n, n /...  8.42 us
    pallas_call x1, Pallas kernels, pivot_two(): pl.pallas_call(pivot_two_kernel, out_shape=[sd(2 * half, half), sd(half,...  8.33 us
    pallas_call x1, Pallas kernels, kept_products(): pl.pallas_call(kept_kernel, out_shape=outs, in_specs=[smem, vmem, vmem, a...  5.08 us
    pallas_call x2, Pallas kernels, final_rows(): pl.pallas_call(kernel, out_shape=jax.ShapeDtypeStruct((2 * HALF, 2 * PW),...  2.8 us
  transfers between devices with their start and end apart: 19, of which 10 were waited for; matrix products, arithmetic and copies ran while one was open for 2% of the time, Pallas kernels for 18%

profile of v4, /device:TPU:0, one launch (start us, length us, event | category | flops | bytes accessed | tf_op | source)
XLA Modules:
  0.0 124.9 jit_solution(6308518143408446579)
XLA Ops:
  0.7 0.1 pad_add_fusion.ids_ref
  0.7 33.6 %scen_solve.1 = (bf16[512,768]{1,0:T(8,128)(2,1)S(1)}, f32[320,512]{1,0:T(8,128)S(1)}, f32[2,2,2,96,512]{4,3,2,1,0:T(8,128)}, f32[2,2,2,96,512]{4,3,2,1,0:T(8,128)}, f32[2,2,2,88,512]{4,3,2,1,0:T(8,128)}) custom-call(s32[2]{0:T(128)S(1)} %pad_add_fusion.ids_ref, s32[1]{0:T(128)S(6)} %copy.6.act_ref, bf16[1,768,768]{2,1,0:T(8,128)(2,1)} %k_ref.1, ...), custom_call_target="tpu_custom_call" | custom-call | tf_op jit(solution)/shard_map/scen_solve/pallas_call | solution.py:224
  34.4 0.5 collective-permute-start
  34.9 0.1 collective-permute-start.1
  35.0 0.4 collective-permute-start.2
  35.4 5.1 %kept_products.1 = (f32[2,2,2,96,512]{4,3,2,1,0:T(8,128)S(1)}, f32[2,2,2,96,512]{4,3,2,1,0:T(8,128)S(1)}, f32[2,2,2,88,512]{4,3,2,1,0:T(8,128)S(1)}) custom-call(s32[2]{0:T(128)S(1)} %pad_add_fusion.ids_ref, bf16[512,768]{1,0:T(8,128)(2,1)S(1)} %get-tuple-element.50.xt_ref, f32[320,512]{1,0:T(8,128)S(1)} %get-tuple-element.51.packed_ref, ...), custom_call_target="tpu_custom_call" | custom-call | flops 1610612736 | bytes 11534336 | tf_op jit(solution)/shard_map/kept_products/pallas_call | solution.py:238
  40.5 0.1 fusion.11
  40.6 0.1 fusion.10
  40.8 0.1 fusion.9
  40.9 0.2 slice_add_fusion
  41.1 2.6 %collective-permute-start.3 = (f32[4,96,512]{2,1,0:T(8,128)S(1)}, f32[4,96,512]{2,1,0:T(8,128)S(1)}, u32[]{:S(2)}, u32[]{:S(2)}) collective-permute-start(f32[4,96,512]{2,1,0:T(8,128)S(1)} %slice_add_fusion), channel_id=1, source_target_pairs={{0,8},{4,12},{8,0},{12,4},{16,24},{20,28},{24,16},{28,20},{1,9},{5... | collective-permute-start | bytes 2359304 | tf_op jit(solution)/shard_map/ppermute | solution.py:338
  43.7 0.2 bitcast_add_fusion.1
  43.9 1.6 %collective-permute-start.4 = (f32[4,96,512]{2,1,0:T(8,128)S(1)}, f32[4,96,512]{2,1,0:T(8,128)S(1)}, u32[]{:S(2)}, u32[]{:S(2)}) collective-permute-start(f32[4,96,512]{2,1,0:T(8,128)S(1)} %bitcast_add_fusion.1), channel_id=1, source_target_pairs={{0,16},{4,20},{8,24},{12,28},{16,0},{20,4},{24,8},{28,12},{1,17},{... | collective-permute-start | bytes 2359304 | tf_op jit(solution)/shard_map/ppermute | solution.py:338
  45.5 0.1 bitcast_add_fusion.4
  45.6 1.6 %collective-permute-start.5 = (f32[4,88,512]{2,1,0:T(8,128)S(1)}, f32[4,88,512]{2,1,0:T(8,128)S(1)}, u32[]{:S(2)}, u32[]{:S(2)}) collective-permute-start(f32[4,88,512]{2,1,0:T(8,128)S(1)} %bitcast_add_fusion.4), channel_id=1, source_target_pairs={{0,1},{1,0},{2,3},{3,2},{4,5},{5,4},{6,7},{7,6},{8,9},{9,8},{10,11... | collective-permute-start | bytes 2162696 | tf_op jit(solution)/shard_map/ppermute | solution.py:338
  47.3 0.4 bitcast_add_fusion
  47.6 0.2 bitcast_add_fusion.3
  47.8 14.1 %collective-permute-done.3 = f32[4,96,512]{2,1,0:T(8,128)S(1)} collective-permute-done((f32[4,96,512]{2,1,0:T(8,128)S(1)}, f32[4,96,512]{2,1,0:T(8,128)S(1)}, u32[]{:S(2)}, u32[]{:S(2)}) %collective-permute-start.3) | collective-permute-done | bytes 786464 | tf_op jit(solution)/shard_map/ppermute | solution.py:338
  61.9 0.1 slice_add_fusion.3
  61.9 1.8 %collective-permute-start.6 = (f32[2,96,512]{2,1,0:T(8,128)S(1)}, f32[2,96,512]{2,1,0:T(8,128)S(1)}, u32[]{:S(2)}, u32[]{:S(2)}) collective-permute-start(f32[2,96,512]{2,1,0:T(8,128)S(1)} %slice_add_fusion.3), channel_id=1, source_target_pairs={{0,16},{4,20},{8,24},{12,28},{16,0},{20,4},{24,8},{28,12},{1,17},{... | collective-permute-start | bytes 1179656 | tf_op jit(solution)/shard_map/ppermute | solution.py:338
  63.8 0.1 slice_add_fusion.2
  63.8 1.6 %collective-permute-start.8 = (f32[2,96,512]{2,1,0:T(8,128)S(1)}, f32[2,96,512]{2,1,0:T(8,128)S(1)}, u32[]{:S(2)}, u32[]{:S(2)}) collective-permute-start(f32[2,96,512]{2,1,0:T(8,128)S(1)} %slice_add_fusion.2), channel_id=1, source_target_pairs={{0,1},{1,0},{2,3},{3,2},{4,5},{5,4},{6,7},{7,6},{8,9},{9,8},{10,11... | collective-permute-start | bytes 1179656 | tf_op jit(solution)/shard_map/ppermute | solution.py:338
  65.5 1.6 %collective-permute-start.9 = (f32[2,88,512]{2,1,0:T(8,128)S(1)}, f32[2,88,512]{2,1,0:T(8,128)S(1)}, u32[]{:S(2)}, u32[]{:S(2)}) collective-permute-start(f32[2,88,512]{2,1,0:T(8,128)S(1)} %slice_add_fusion.6), channel_id=1, source_target_pairs={{0,8},{4,12},{8,0},{12,4},{16,24},{20,28},{24,16},{28,20},{1,9},{5... | collective-permute-start | bytes 1081352 | tf_op jit(solution)/shard_map/ppermute | solution.py:338
  67.1 0.1 slice_add_fusion.1
  67.2 0.1 slice_add_fusion.4
  67.3 5.6 %collective-permute-done.6 = f32[2,96,512]{2,1,0:T(8,128)S(1)} collective-permute-done((f32[2,96,512]{2,1,0:T(8,128)S(1)}, f32[2,96,512]{2,1,0:T(8,128)S(1)}, u32[]{:S(2)}, u32[]{:S(2)}) %collective-permute-start.6) | collective-permute-done | bytes 393248 | tf_op jit(solution)/shard_map/ppermute | solution.py:338
  73.0 1.7 %collective-permute-start.7 = (f32[112,512]{1,0:T(8,128)S(1)}, f32[112,512]{1,0:T(8,128)S(1)}, u32[]{:S(2)}, u32[]{:S(2)}) collective-permute-start(f32[112,512]{1,0:T(8,128)S(1)} %pad_maximum_fusion.1), channel_id=1, source_target_pairs={{0,1},{1,0},{2,3},{3,2},{4,5},{5,4},{6,7},{7,6},{8,9},{9,8},{10,11... | collective-permute-start | bytes 688136 | tf_op jit(solution)/shard_map/ppermute | solution.py:338
  74.7 1.6 %collective-permute-start.11 = (f32[96,512]{1,0:T(8,128)S(1)}, f32[96,512]{1,0:T(8,128)S(1)}, u32[]{:S(2)}, u32[]{:S(2)}) collective-permute-start(f32[96,512]{1,0:T(8,128)S(1)} %fusion.1), channel_id=1, source_target_pairs={{0,8},{4,12},{8,0},{12,4},{16,24},{20,28},{24,16},{28,20},{1,9},{5... | collective-permute-start | bytes 589832 | tf_op jit(solution)/shard_map/ppermute | solution.py:338
  76.4 3.1 %collective-permute-done.7 = f32[112,512]{1,0:T(8,128)S(1)} collective-permute-done((f32[112,512]{1,0:T(8,128)S(1)}, f32[112,512]{1,0:T(8,128)S(1)}, u32[]{:S(2)}, u32[]{:S(2)}) %collective-permute-start.7) | collective-permute-done | bytes 229408 | tf_op jit(solution)/shard_map/ppermute | solution.py:338
  79.6 2.5 %collective-permute-start.10 = (f32[40,512]{1,0:T(8,128)S(1)}, f32[40,512]{1,0:T(8,128)S(1)}, u32[]{:S(2)}, u32[]{:S(2)}) collective-permute-start(f32[40,512]{1,0:T(8,128)S(1)} %maximum_add_fusion), channel_id=1, source_target_pairs={{0,2},{1,3},{2,0},{3,1},{4,6},{5,7},{6,4},{7,5},{8,10},{9,11},{10,... | collective-permute-start | bytes 245768 | tf_op jit(solution)/shard_map/ppermute | solution.py:338
  82.1 1.5 %collective-permute-start.12 = (f32[88,512]{1,0:T(8,128)S(1)}, f32[88,512]{1,0:T(8,128)S(1)}, u32[]{:S(2)}, u32[]{:S(2)}) collective-permute-start(f32[88,512]{1,0:T(8,128)S(1)} %fusion.3), channel_id=1, source_target_pairs={{0,16},{4,20},{8,24},{12,28},{16,0},{20,4},{24,8},{28,12},{1,17},{... | collective-permute-start | bytes 540680 | tf_op jit(solution)/shard_map/ppermute | solution.py:338
  83.6 1.4 %collective-permute-done.10 = f32[40,512]{1,0:T(8,128)S(1)} collective-permute-done((f32[40,512]{1,0:T(8,128)S(1)}, f32[40,512]{1,0:T(8,128)S(1)}, u32[]{:S(2)}, u32[]{:S(2)}) %collective-permute-start.10) | collective-permute-done | bytes 81952 | tf_op jit(solution)/shard_map/ppermute | solution.py:338
  85.1 2.5 %collective-permute-done.12 = f32[88,512]{1,0:T(8,128)S(1)} collective-permute-done((f32[88,512]{1,0:T(8,128)S(1)}, f32[88,512]{1,0:T(8,128)S(1)}, u32[]{:S(2)}, u32[]{:S(2)}) %collective-permute-start.12) | collective-permute-done | bytes 180256 | tf_op jit(solution)/shard_map/ppermute | solution.py:338
  87.6 0.5 collective-permute-start.17
  88.2 1.3 %collective-permute-done.13 = f32[40,512]{1,0:T(8,128)S(1)} collective-permute-done((f32[40,512]{1,0:T(8,128)S(1)}, f32[40,512]{1,0:T(8,128)S(1)}, u32[]{:S(2)}, u32[]{:S(2)}) %collective-permute-start.13) | collective-permute-done | bytes 81952 | tf_op jit(solution)/shard_map/ppermute | solution.py:338
  89.5 1.4 %collective-permute-start.14 = (f32[80,512]{1,0:T(8,128)S(1)}, f32[80,512]{1,0:T(8,128)S(1)}, u32[]{:S(2)}, u32[]{:S(2)}) collective-permute-start(f32[80,512]{1,0:T(8,128)S(1)} %constant_dynamic-update-slice_fusion.refs_0_), channel_id=1, source_target_pairs={{0,8},{4,12},{8,0},{12,4},{16,24},{20,28},{24,16},{28,20},{1,9},{5... | collective-permute-start | bytes 491528 | tf_op jit(solution)/shard_map/ppermute | solution.py:338
  90.9 1.5 %collective-permute-start.15 = (f32[80,512]{1,0:T(8,128)S(1)}, f32[80,512]{1,0:T(8,128)S(1)}, u32[]{:S(2)}, u32[]{:S(2)}) collective-permute-start(f32[80,512]{1,0:T(8,128)S(1)} %constant_dynamic-update-slice_fusion.refs_0_), channel_id=1, source_target_pairs={{0,16},{4,20},{8,24},{12,28},{16,0},{20,4},{24,8},{28,12},{1,17},{... | collective-permute-start | bytes 491528 | tf_op jit(solution)/shard_map/ppermute | solution.py:338
  92.4 0.6 collective-permute-start.16
  93.0 3.6 %collective-permute-done.14.refs_1_ = f32[80,512]{1,0:T(8,128)S(1)} collective-permute-done((f32[80,512]{1,0:T(8,128)S(1)}, f32[80,512]{1,0:T(8,128)S(1)}, u32[]{:S(2)}, u32[]{:S(2)}) %collective-permute-start.14) | collective-permute-done | bytes 163872 | tf_op jit(solution)/shard_map/ppermute | solution.py:338
  96.6 3.7 %collective-permute-done.15.refs_2_ = f32[80,512]{1,0:T(8,128)S(1)} collective-permute-done((f32[80,512]{1,0:T(8,128)S(1)}, f32[80,512]{1,0:T(8,128)S(1)}, u32[]{:S(2)}, u32[]{:S(2)}) %collective-permute-start.15) | collective-permute-done | bytes 163872 | tf_op jit(solution)/shard_map/ppermute | solution.py:338
  100.3 8.4 %pivot_one.1 = (f32[256,256]{1,0:T(8,128)S(1)}, f32[512,256]{1,0:T(8,128)S(1)}, f32[256,256]{1,0:T(8,128)S(1)}, f32[256,256]{1,0:T(8,128)S(1)}) custom-call(s32[2]{0:T(128)S(1)} %pad_add_fusion.ids_ref, f32[1,512]{1,0:T(1,128)S(1)} %bitcast.34, f32[80,512]{1,0:T(8,128)S(1)} %constant_dynamic-update-slice_fusion.refs_0_, ...), custom_call_target="tpu_custom_call" | custom-call | flops 1 | bytes 1 | tf_op jit(solution)/shard_map/pivot_one/pallas_call | solution.py:290
  108.7 1.6 %collective-permute-done.17 = f32[256,512]{1,0:T(8,128)S(1)} collective-permute-done((f32[256,512]{1,0:T(8,128)S(1)}, f32[256,512]{1,0:T(8,128)S(1)}, u32[]{:S(2)}, u32[]{:S(2)}) %collective-permute-start.17) | collective-permute-done | bytes 524320 | tf_op jit(solution)/shard_map/ppermute | solution.py:338
  110.4 0.1 fusion.8.mine_ref
  110.5 0.4 collective-permute-start.18
  110.9 8.3 %pivot_two.1 = (f32[512,256]{1,0:T(8,128)S(1)}, f32[256,256]{1,0:T(8,128)S(1)}) custom-call(f32[256,256]{1,0:T(8,128)S(1)} %get-tuple-element.78.wt1_ref, f32[256,256]{1,0:T(8,128)S(1)} %get-tuple-element.79.u_ref, f32[256,256]{1,0:T(8,128)S(1)} %get-tuple-element.82.rest_ref), custom_call_target="tpu_custom_call" | custom-call | flops 1 | bytes 1 | tf_op jit(solution)/shard_map/pivot_two/pallas_call | solution.py:326
  119.2 1.2 owned_rows.2.held_ref
  120.4 2.9 %collective-permute-done.18.other_ref = f32[256,512]{1,0:T(8,128)S(1)} collective-permute-done((f32[256,512]{1,0:T(8,128)S(1)}, f32[256,512]{1,0:T(8,128)S(1)}, u32[]{:S(2)}, u32[]{:S(2)}) %collective-permute-start.18) | collective-permute-done | bytes 524320 | tf_op jit(solution)/shard_map/ppermute | solution.py:338
  123.3 1.6 %owned_rows.3 = f32[512,512]{1,0:T(8,128)} custom-call(s32[2]{0:T(128)S(1)} %pad_add_fusion.ids_ref, f32[256,256]{1,0:T(8,128)S(1)} %get-tuple-element.78.wt1_ref, f32[512,256]{1,0:T(8,128)S(1)} %get-tuple-element.83.wt2_ref, f32[512,256]{1,0:T(8,128)S(1)} %get-tuple-element.84.l1_ref, f32[256,256]{1,0:T(8,128)S(1)} %get-tuple-element.85.l2_ref, ...), custom_call_target="tpu_custom_call" | custom-call | flops 1 | bytes 1 | tf_op jit(solution)/shard_map/owned_rows/pallas_call | solution.py:347
  (34 shorter events, 0.5 us)
Async XLA Ops:
  0.7 34.7 %copy-start = (bf16[1,768,4096]{2,1,0:T(8,128)(2,1)S(1)}, bf16[1,768,4096]{2,1,0:T(8,128)(2,1)}, u32[]{:S(2)}) copy-start(bf16[1,768,4096]{2,1,0:T(8,128)(2,1)} %c_hbm.3) | copy-start | bytes 18874372
  34.4 6.5 %collective-permute-start = (f32[8,96,512]{2,1,0:T(8,128)}, f32[8,96,512]{2,1,0:T(8,128)S(1)}, u32[]{:S(2)}, u32[]{:S(2)}) collective-permute-start(f32[8,96,512]{2,1,0:T(8,128)} %bitcast.36), channel_id=1, source_target_pairs={{0,4},{4,0},{8,12},{12,8},{16,20},{20,16},{24,28},{28,24},{1,5},{5... | collective-permute-start | bytes 4718600 | tf_op jit(solution)/shard_map/ppermute | solution.py:338
  34.9 8.8 %collective-permute-start.1 = (f32[8,96,512]{2,1,0:T(8,128)}, f32[8,96,512]{2,1,0:T(8,128)S(1)}, u32[]{:S(2)}, u32[]{:S(2)}) collective-permute-start(f32[8,96,512]{2,1,0:T(8,128)} %bitcast.35), channel_id=1, source_target_pairs={{0,4},{4,0},{8,12},{12,8},{16,20},{20,16},{24,28},{28,24},{1,5},{5... | collective-permute-start | bytes 4718600 | tf_op jit(solution)/shard_map/ppermute | solution.py:338
  35.0 10.5 %collective-permute-start.2 = (f32[8,88,512]{2,1,0:T(8,128)}, f32[8,88,512]{2,1,0:T(8,128)S(1)}, u32[]{:S(2)}, u32[]{:S(2)}) collective-permute-start(f32[8,88,512]{2,1,0:T(8,128)} %bitcast.37), channel_id=1, source_target_pairs={{0,4},{4,0},{8,12},{12,8},{16,20},{20,16},{24,28},{28,24},{1,5},{5... | collective-permute-start | bytes 4325384 | tf_op jit(solution)/shard_map/ppermute | solution.py:338
  41.1 20.8 %collective-permute-start.3 = (f32[4,96,512]{2,1,0:T(8,128)S(1)}, f32[4,96,512]{2,1,0:T(8,128)S(1)}, u32[]{:S(2)}, u32[]{:S(2)}) collective-permute-start(f32[4,96,512]{2,1,0:T(8,128)S(1)} %slice_add_fusion), channel_id=1, source_target_pairs={{0,8},{4,12},{8,0},{12,4},{16,24},{20,28},{24,16},{28,20},{1,9},{5... | collective-permute-start | bytes 2359304 | tf_op jit(solution)/shard_map/ppermute | solution.py:338
  43.9 19.9 %collective-permute-start.4 = (f32[4,96,512]{2,1,0:T(8,128)S(1)}, f32[4,96,512]{2,1,0:T(8,128)S(1)}, u32[]{:S(2)}, u32[]{:S(2)}) collective-permute-start(f32[4,96,512]{2,1,0:T(8,128)S(1)} %bitcast_add_fusion.1), channel_id=1, source_target_pairs={{0,16},{4,20},{8,24},{12,28},{16,0},{20,4},{24,8},{28,12},{1,17},{... | collective-permute-start | bytes 2359304 | tf_op jit(solution)/shard_map/ppermute | solution.py:338
  45.6 19.9 %collective-permute-start.5 = (f32[4,88,512]{2,1,0:T(8,128)S(1)}, f32[4,88,512]{2,1,0:T(8,128)S(1)}, u32[]{:S(2)}, u32[]{:S(2)}) collective-permute-start(f32[4,88,512]{2,1,0:T(8,128)S(1)} %bitcast_add_fusion.4), channel_id=1, source_target_pairs={{0,1},{1,0},{2,3},{3,2},{4,5},{5,4},{6,7},{7,6},{8,9},{9,8},{10,11... | collective-permute-start | bytes 2162696 | tf_op jit(solution)/shard_map/ppermute | solution.py:338
  61.9 10.9 %collective-permute-start.6 = (f32[2,96,512]{2,1,0:T(8,128)S(1)}, f32[2,96,512]{2,1,0:T(8,128)S(1)}, u32[]{:S(2)}, u32[]{:S(2)}) collective-permute-start(f32[2,96,512]{2,1,0:T(8,128)S(1)} %slice_add_fusion.3), channel_id=1, source_target_pairs={{0,16},{4,20},{8,24},{12,28},{16,0},{20,4},{24,8},{28,12},{1,17},{... | collective-permute-start | bytes 1179656 | tf_op jit(solution)/shard_map/ppermute | solution.py:338
  63.8 10.8 %collective-permute-start.8 = (f32[2,96,512]{2,1,0:T(8,128)S(1)}, f32[2,96,512]{2,1,0:T(8,128)S(1)}, u32[]{:S(2)}, u32[]{:S(2)}) collective-permute-start(f32[2,96,512]{2,1,0:T(8,128)S(1)} %slice_add_fusion.2), channel_id=1, source_target_pairs={{0,1},{1,0},{2,3},{3,2},{4,5},{5,4},{6,7},{7,6},{8,9},{9,8},{10,11... | collective-permute-start | bytes 1179656 | tf_op jit(solution)/shard_map/ppermute | solution.py:338
  65.5 10.7 %collective-permute-start.9 = (f32[2,88,512]{2,1,0:T(8,128)S(1)}, f32[2,88,512]{2,1,0:T(8,128)S(1)}, u32[]{:S(2)}, u32[]{:S(2)}) collective-permute-start(f32[2,88,512]{2,1,0:T(8,128)S(1)} %slice_add_fusion.6), channel_id=1, source_target_pairs={{0,8},{4,12},{8,0},{12,4},{16,24},{20,28},{24,16},{28,20},{1,9},{5... | collective-permute-start | bytes 1081352 | tf_op jit(solution)/shard_map/ppermute | solution.py:338
  73.0 6.6 %collective-permute-start.7 = (f32[112,512]{1,0:T(8,128)S(1)}, f32[112,512]{1,0:T(8,128)S(1)}, u32[]{:S(2)}, u32[]{:S(2)}) collective-permute-start(f32[112,512]{1,0:T(8,128)S(1)} %pad_maximum_fusion.1), channel_id=1, source_target_pairs={{0,1},{1,0},{2,3},{3,2},{4,5},{5,4},{6,7},{7,6},{8,9},{9,8},{10,11... | collective-permute-start | bytes 688136 | tf_op jit(solution)/shard_map/ppermute | solution.py:338
  74.7 10.3 %collective-permute-start.11 = (f32[96,512]{1,0:T(8,128)S(1)}, f32[96,512]{1,0:T(8,128)S(1)}, u32[]{:S(2)}, u32[]{:S(2)}) collective-permute-start(f32[96,512]{1,0:T(8,128)S(1)} %fusion.1), channel_id=1, source_target_pairs={{0,8},{4,12},{8,0},{12,4},{16,24},{20,28},{24,16},{28,20},{1,9},{5... | collective-permute-start | bytes 589832 | tf_op jit(solution)/shard_map/ppermute | solution.py:338
  79.5 20.8 %copy-start.1 = (f32[512]{0:T(512)S(1)}, f32[512]{0:T(512)}, u32[]{:S(2)}) copy-start(f32[512]{0:T(512)} %param.7) | copy-start | bytes 6148
  79.6 5.4 %collective-permute-start.10 = (f32[40,512]{1,0:T(8,128)S(1)}, f32[40,512]{1,0:T(8,128)S(1)}, u32[]{:S(2)}, u32[]{:S(2)}) collective-permute-start(f32[40,512]{1,0:T(8,128)S(1)} %maximum_add_fusion), channel_id=1, source_target_pairs={{0,2},{1,3},{2,0},{3,1},{4,6},{5,7},{6,4},{7,5},{8,10},{9,11},{10,... | collective-permute-start | bytes 245768 | tf_op jit(solution)/shard_map/ppermute | solution.py:338
  82.1 5.5 %collective-permute-start.12 = (f32[88,512]{1,0:T(8,128)S(1)}, f32[88,512]{1,0:T(8,128)S(1)}, u32[]{:S(2)}, u32[]{:S(2)}) collective-permute-start(f32[88,512]{1,0:T(8,128)S(1)} %fusion.3), channel_id=1, source_target_pairs={{0,16},{4,20},{8,24},{12,28},{16,0},{20,4},{24,8},{28,12},{1,17},{... | collective-permute-start | bytes 540680 | tf_op jit(solution)/shard_map/ppermute | solution.py:338
  87.6 22.7 %collective-permute-start.17 = (f32[256,512]{1,0:T(8,128)S(1)}, f32[256,512]{1,0:T(8,128)S(1)}, u32[]{:S(2)}, u32[]{:S(2)}) collective-permute-start(f32[256,512]{1,0:T(8,128)S(1)} %pad_maximum_fusion), channel_id=1, source_target_pairs={{0,2},{1,3},{2,0},{3,1},{4,6},{5,7},{6,4},{7,5},{8,10},{9,11},{10,... | collective-permute-start | bytes 1572872 | tf_op jit(solution)/shard_map/ppermute | solution.py:338
  88.2 1.3 %collective-permute-start.13 = (f32[40,512]{1,0:T(8,128)S(1)}, f32[40,512]{1,0:T(8,128)S(1)}, u32[]{:S(2)}, u32[]{:S(2)}) collective-permute-start(f32[40,512]{1,0:T(8,128)S(1)} %add.136), channel_id=1, source_target_pairs={{0,4},{4,0},{8,12},{12,8},{16,20},{20,16},{24,28},{28,24},{1,5},{5... | collective-permute-start | bytes 245768 | tf_op jit(solution)/shard_map/ppermute | solution.py:338
  89.5 7.1 %collective-permute-start.14 = (f32[80,512]{1,0:T(8,128)S(1)}, f32[80,512]{1,0:T(8,128)S(1)}, u32[]{:S(2)}, u32[]{:S(2)}) collective-permute-start(f32[80,512]{1,0:T(8,128)S(1)} %constant_dynamic-update-slice_fusion.refs_0_), channel_id=1, source_target_pairs={{0,8},{4,12},{8,0},{12,4},{16,24},{20,28},{24,16},{28,20},{1,9},{5... | collective-permute-start | bytes 491528 | tf_op jit(solution)/shard_map/ppermute | solution.py:338
  90.9 9.4 %collective-permute-start.15 = (f32[80,512]{1,0:T(8,128)S(1)}, f32[80,512]{1,0:T(8,128)S(1)}, u32[]{:S(2)}, u32[]{:S(2)}) collective-permute-start(f32[80,512]{1,0:T(8,128)S(1)} %constant_dynamic-update-slice_fusion.refs_0_), channel_id=1, source_target_pairs={{0,16},{4,20},{8,24},{12,28},{16,0},{20,4},{24,8},{28,12},{1,17},{... | collective-permute-start | bytes 491528 | tf_op jit(solution)/shard_map/ppermute | solution.py:338
  92.4 7.9 %collective-permute-start.16 = (f32[80,512]{1,0:T(8,128)S(1)}, f32[80,512]{1,0:T(8,128)S(1)}, u32[]{:S(2)}, u32[]{:S(2)}) collective-permute-start(f32[80,512]{1,0:T(8,128)S(1)} %constant_dynamic-update-slice_fusion.refs_0_), channel_id=1, source_target_pairs={{0,24},{4,28},{8,16},{12,20},{16,8},{20,12},{24,0},{28,4},{1,25},{... | collective-permute-start | bytes 491528 | tf_op jit(solution)/shard_map/ppermute | solution.py:338
  110.5 12.8 %collective-permute-start.18 = (f32[256,512]{1,0:T(8,128)S(1)}, f32[256,512]{1,0:T(8,128)S(1)}, u32[]{:S(2)}, u32[]{:S(2)}) collective-permute-start(f32[256,512]{1,0:T(8,128)S(1)} %fusion.8.mine_ref), channel_id=1, source_target_pairs={{0,1},{1,0},{2,3},{3,2},{4,5},{5,4},{6,7},{7,6},{8,9},{9,8},{10,11... | collective-permute-start | bytes 1572872 | tf_op jit(solution)/shard_map/ppermute | solution.py:338
